TPU v7x, 1024 devices: a whole 4x8x16 slice. The times are simulated.
1024 devices in a mesh: group: 16 (over y, core), expert: 64 (over x, z).
Axes of the slice: x: 4, y: 8, z: 16, core: 2. Of those that a mesh axis runs over, the one named last changes fastest.
Arguments:
- tokens: bfloat16 [4096, 4096], P(('group', 'expert')), may hold values from -6 to 6
- expert_ids: int32 [4096, 8], P(('group', 'expert')), may hold values from 0 to 127, as said below
- gates: bfloat16 [4096, 8], P(('group', 'expert')), may hold values from 0.099609375 to 1
- gate_weight: bfloat16 [1024, 4096, 128], P(('group', 'expert')), may hold values from -0.09375 to 0.09375
- up_weight: bfloat16 [1024, 4096, 128], P(('group', 'expert')), may hold values from -0.09375 to 0.09375
- down_weight: bfloat16 [1024, 128, 4096], P(('group', 'expert')), may hold values from -0.1875 to 0.1875
Outputs:
- mixed: bfloat16 [4096, 4096], P(('group', 'expert'))
Inputs may be any that keep to these rules, and one draw needn't show every extreme that they name: `expert_ids`: each token names 8 different experts lying in exactly 4 groups, with one to 4 of them in each of those groups. The tokens of one device use any one group at most 1 times, and every device reaches 1 for some group. Among the tokens of the 16 devices that share one index along expert, at most 8 name any one expert, and in every draw some expert is named exactly that often.
All inputs are finite; a program needn't handle non-finite values.
Results may differ from a plain program's by a relative error of at most 0.006.
Values may be sent and summed in bfloat16 or wider, within the bound.
No kernel may reach another device: no remote copies, remote signals or barrier semaphores. Data moves between devices by JAX's collectives and lax.ppermute only.
A program may use at most 32 MiB of HBM per device.

v0:
```python
import jax
import jax.numpy as jnp
from jax import lax
from jax.sharding import PartitionSpec as P

EXP_GROUP = 8
TOP = 8
TOPG = 4


def on_device(tokens, expert_ids, gates, gate_weight, up_weight, down_weight):
    groups = lax.axis_size("group")
    columns = lax.axis_size("expert")
    tok_rows, features = tokens.shape
    slices = columns // EXP_GROUP
    capacity = 2 * tok_rows
    group_slots = (tok_rows * TOPG + groups - 1) // groups
    most_picks = TOP - TOPG
    group_of = expert_ids // EXP_GROUP
    local_of = expert_ids % EXP_GROUP
    group_hit = (group_of[:, :, None] == jnp.arange(groups, dtype=jnp.int32)[None, None, :]).astype(
        jnp.float32
    )
    local_hit = (
        local_of[:, :, None] == jnp.arange(EXP_GROUP, dtype=jnp.int32)[None, None, :]
    ).astype(jnp.float32)
    chosen = jnp.sum(group_hit, axis=1) > 0
    chosen_int = chosen.astype(jnp.int32)
    rank_of = jnp.cumsum(chosen_int, axis=0) - chosen_int
    slot_hit = chosen.T[:, None, :] & (
        rank_of.T[:, None, :] == jnp.arange(group_slots, dtype=jnp.int32)[None, :, None]
    )
    home_select = slot_hit.astype(jnp.float32)
    send_rows = jnp.einsum(
        "gct,td->gcd", slot_hit.astype(jnp.bfloat16), tokens, preferred_element_type=jnp.float32
    ).astype(jnp.bfloat16)
    gate_by_token = jnp.einsum("tpg,tpk,tp->gtk", group_hit, local_hit, gates.astype(jnp.float32))
    gate_table = jnp.einsum(
        "gct,gtk->gck", home_select, gate_by_token, precision=lax.Precision.HIGHEST
    ).astype(jnp.bfloat16)
    arrived, arrived_gates = (
        lax.all_to_all(send_rows, "group", split_axis=0, concat_axis=0, tiled=True),
        lax.all_to_all(gate_table, "group", split_axis=0, concat_axis=0, tiled=True),
    )
    arrivals = arrived.reshape(groups * group_slots, features)
    arrival_gates = arrived_gates.reshape(groups * group_slots, EXP_GROUP).astype(jnp.float32)
    picked = arrival_gates > 0
    picked_int = picked.astype(jnp.int32)
    slot_of = jnp.cumsum(picked_int, axis=0) - picked_int
    slot_match = slot_of.T[:, None, :] == jnp.arange(capacity, dtype=jnp.int32)[None, :, None]
    selector = (picked.T[:, None, :] & slot_match).astype(jnp.bfloat16)
    outgoing = jnp.einsum(
        "kca,ad->kcd", selector, arrivals, preferred_element_type=jnp.float32
    ).astype(jnp.bfloat16)
    outgoing = jnp.broadcast_to(outgoing[:, None], (EXP_GROUP, slices, capacity, features)).reshape(
        columns, capacity, features
    )
    received = lax.all_to_all(outgoing, "expert", split_axis=0, concat_axis=0, tiled=True)
    stacked = received.reshape(-1, features)
    gate_act = jnp.dot(stacked, gate_weight[0], preferred_element_type=jnp.float32)
    up_act = jnp.dot(stacked, up_weight[0], preferred_element_type=jnp.float32)
    hidden = (jax.nn.silu(gate_act) * up_act).astype(jnp.bfloat16)
    partial_rows = jnp.dot(hidden, down_weight[0], preferred_element_type=jnp.float32).astype(
        jnp.bfloat16
    )
    returned = lax.all_to_all(
        partial_rows.reshape(received.shape), "expert", split_axis=0, concat_axis=0, tiled=True
    )
    expert_out = jnp.sum(
        returned.reshape(EXP_GROUP, slices, capacity, features), axis=1, dtype=jnp.float32
    )
    fetch_index = jnp.where(
        picked, jnp.arange(EXP_GROUP, dtype=jnp.int32)[None, :] * capacity + slot_of, 0
    )
    fetched = jnp.take(
        expert_out.reshape(EXP_GROUP * capacity, features), fetch_index.reshape(-1), axis=0
    )
    weighted = (
        fetched.reshape(groups * group_slots, EXP_GROUP, features) * arrival_gates[:, :, None]
    )
    pick_rank = jnp.cumsum(picked_int, axis=1) - picked_int
    pick_match = (
        picked[:, :, None]
        & (pick_rank[:, :, None] == jnp.arange(most_picks, dtype=jnp.int32)[None, None, :])
    ).astype(jnp.float32)
    per_pick = jnp.einsum("akq,akd->aqd", pick_match, weighted, precision=lax.Precision.HIGHEST)
    returned_picks = lax.all_to_all(per_pick, "group", split_axis=0, concat_axis=0, tiled=True)
    back_home = jnp.sum(returned_picks.reshape(groups, group_slots, most_picks, features), axis=2)
    result = jnp.einsum("gct,gcd->td", home_select, back_home, precision=lax.Precision.HIGHEST)
    return result.astype(jnp.bfloat16)


def solution(mesh):
    in_specs = (
        P(("group", "expert"), None),
        P(("group", "expert"), None),
        P(("group", "expert"), None),
        P(("group", "expert"), None, None),
        P(("group", "expert"), None, None),
        P(("group", "expert"), None, None),
    )
    out_specs = P(("group", "expert"), None)
    return jax.shard_map(
        on_device, mesh=mesh, in_specs=in_specs, out_specs=out_specs, check_vma=False
    )
```

profile of v0, /device:TPU:1, one launch (start us, length us, event | category | flops | bytes accessed | tf_op | source)
XLA Modules:
  0.0 491.3 jit_solution(29753176926696514)
XLA Ops:
  0.0 0.8 add_select_fusion
  0.9 0.9 fusion.16
  1.8 0.7 copy.25
  2.5 17.4 %all-to-all-start = ((bf16[16,1,8]{2,1,0:T(2,128)(2,1)}), bf16[16,1,8]{2,1,0:T(2,128)(2,1)S(1)}, u32[]{:S(2)}, u32[]{:S(2)}) async-start(bf16[16,1,8]{2,1,0:T(2,128)(2,1)} %copy.25), calls=%async_computation | async-start | bytes 16384 | tf_op jit(solution)/shard_map/all_to_all | solution.py:43
  19.9 1.0 fusion.1
  20.9 0.6 broadcast.127
  21.5 0.7 reduce.4
  22.2 0.7 reshape.164
  22.9 4.0 all-to-all-done
  26.9 4.0 all-to-all-start.1
  31.4 8.7 %all-to-all-done.1 = bf16[16,2,2048]{2,1,0:T(2,128)(2,1)S(1)} async-done(((bf16[16,2,2048]{2,1,0:T(2,128)(2,1)}), bf16[16,2,2048]{2,1,0:T(2,128)(2,1)S(1)}, u32[]{:S(2)}, u32[]{:S(2)}) %all-to-all-start.1) | async-done | bytes 131104 | tf_op jit(solution)/shard_map/all_to_all | solution.py:42
  40.5 0.5 broadcast_in_dim.17
  41.0 199.9 %all_to_all.25 = bf16[64,8,4096]{2,1,0:T(8,128)(2,1)S(1)} all-to-all(bf16[64,8,4096]{2,1,0:T(8,128)(2,1)S(1)} %bitcast.72), channel_id=1, replica_groups=mesh['group'=16,'expert'=64] {'expert'}, dimensions={0} | all-to-all | bytes 8388608 | tf_op jit(solution)/shard_map/all_to_all | solution.py:58
  241.0 2.0 copy-done.1
  242.9 1.2 fusion.4
  244.2 8.6 %fusion = bf16[64,8,4096]{2,1,0:T(8,128)(2,1)} fusion(bf16[1,128,4096]{2,1,0:T(8,128)(2,1)S(1)} %copy-done, bf16[64,8,4096]{2,1,0:T(8,128)(2,1)} %copy-done.1, bf16[1,4096,128]{2,1,0:T(8,128)(2,1)S(1)} %copy-done.3, f32[512,128]{1,0:T(8,128)S(1)} %fusion.4), kind=kOutput, calls=%fused_computation.3 | convolution fusion | flops 1076232192 | bytes 10747904 | tf_op jit(solution)/shard_map/dot_general | solution.py:63
  252.8 8.8 %all-to-all-start.3 = ((bf16[64,8,4096]{2,1,0:T(8,128)(2,1)}), bf16[64,8,4096]{2,1,0:T(8,128)(2,1)}, u32[]{:S(2)}, u32[]{:S(2)}) async-start(bf16[64,8,4096]{2,1,0:T(8,128)(2,1)} %fusion), calls=%async_computation.3 | async-start | bytes 8388608 | tf_op jit(solution)/shard_map/all_to_all | solution.py:66
  262.1 181.8 %all-to-all-done.3 = bf16[64,8,4096]{2,1,0:T(8,128)(2,1)} async-done(((bf16[64,8,4096]{2,1,0:T(8,128)(2,1)}), bf16[64,8,4096]{2,1,0:T(8,128)(2,1)}, u32[]{:S(2)}, u32[]{:S(2)}) %all-to-all-start.3) | async-done | bytes 4194336 | tf_op jit(solution)/shard_map/all_to_all | solution.py:66
  443.9 3.0 convert_reduce_fusion
  446.9 2.6 gather_fusion
  449.5 2.9 fusion.7
  452.3 37.5 %all_to_all.26 = f32[16,4,4096]{2,1,0:T(4,128)S(1)} all-to-all(f32[16,4,4096]{2,1,0:T(4,128)S(1)} %fusion.7), channel_id=1, replica_groups=mesh['group'=16,'expert'=64] {'group'}, dimensions={0} | all-to-all | bytes 2097152 | tf_op jit(solution)/shard_map/all_to_all | solution.py:87
  489.8 0.6 reduce_sum.29
  490.4 0.8 convolution_convert_fusion.3
  (32 shorter events, 1.5 us)
Async XLA Ops:
  0.0 244.2 %copy-start = (bf16[1,128,4096]{2,1,0:T(8,128)(2,1)S(1)}, bf16[1,128,4096]{2,1,0:T(8,128)(2,1)}, u32[]{:S(2)}) copy-start(bf16[1,128,4096]{2,1,0:T(8,128)(2,1)} %param.11) | copy-start | bytes 3145732
  2.5 24.4 %all-to-all-start = ((bf16[16,1,8]{2,1,0:T(2,128)(2,1)}), bf16[16,1,8]{2,1,0:T(2,128)(2,1)S(1)}, u32[]{:S(2)}, u32[]{:S(2)}) async-start(bf16[16,1,8]{2,1,0:T(2,128)(2,1)} %copy.25), calls=%async_computation | async-start | bytes 16384 | tf_op jit(solution)/shard_map/all_to_all | solution.py:43
  26.9 13.2 %all-to-all-start.1 = ((bf16[16,2,2048]{2,1,0:T(2,128)(2,1)}), bf16[16,2,2048]{2,1,0:T(2,128)(2,1)S(1)}, u32[]{:S(2)}, u32[]{:S(2)}) async-start(bf16[16,2,2048]{2,1,0:T(2,128)(2,1)} %reshape.164), calls=%async_computation.1 | async-start | bytes 262144 | tf_op jit(solution)/shard_map/all_to_all | solution.py:42
  41.0 201.9 %copy-start.2 = (bf16[1,4096,128]{2,1,0:T(8,128)(2,1)S(1)}, bf16[1,4096,128]{2,1,0:T(8,128)(2,1)}, u32[]{:S(2)}) copy-start(bf16[1,4096,128]{2,1,0:T(8,128)(2,1)} %param.9) | copy-start | bytes 3145732
  241.0 2.0 copy-start.1
  242.9 1.3 copy-start.3
  252.8 191.1 %all-to-all-start.3 = ((bf16[64,8,4096]{2,1,0:T(8,128)(2,1)}), bf16[64,8,4096]{2,1,0:T(8,128)(2,1)}, u32[]{:S(2)}, u32[]{:S(2)}) async-start(bf16[64,8,4096]{2,1,0:T(8,128)(2,1)} %fusion), calls=%async_computation.3 | async-start | bytes 8388608 | tf_op jit(solution)/shard_map/all_to_all | solution.py:66
where the time goes:
time: 492 us; the launch traced here: 491 us
  blocking collectives  237 us (48%)
  waiting for transfers between devices  194 us (39%)
  starting transfers between devices  30.2 us (6%)
  matrix products  15.7 us (3%)
  local copies, waits for them, and re-layouts  7.86 us (2%)
  other arithmetic  5.47 us (1%)
    all_to_all x1, blocking collectives, on_device(): lax.all_to_all(outgoing, 'expert', split_axis=0, concat_axis=0, tiled=True)  200 us
    all_to_all x1, waiting for transfers between devices, on_device(): lax.all_to_all(partial_rows.reshape(received.shape), 'expert', split_axis...  182 us
    all_to_all x1, blocking collectives, on_device(): lax.all_to_all(per_pick, 'group', split_axis=0, concat_axis=0, tiled=True)  37.5 us
    all_to_all x1, starting transfers between devices, on_device(): lax.all_to_all(gate_table, 'group', split_axis=0, concat_axis=0, tiled=True)  17.4 us
  transfers between devices with their start and end apart: 3, of which 3 were waited for; matrix products, arithmetic and copies ran while one was open for 1% of the time, Pallas kernels for 0%

commit v1 on v0

v1 whole, which is shorter than its diff:
```python
import jax
import jax.numpy as jnp
from jax import lax
from jax.sharding import Mesh, PartitionSpec as P

EXP_GROUP = 8
LANES = 128
X_CHIPS = 4
FRONT = 2048


def on_device(tokens, expert_ids, gates, gate_weight, up_weight, down_weight):
    groups = lax.axis_size("group")
    nx = lax.axis_size("x")
    nz = lax.axis_size("z")
    slices = nx * nz // EXP_GROUP
    features = tokens.shape[1]
    units = gate_weight.shape[2]
    x_me = lax.axis_index("x")
    to_right = [(i, (i + 1) % nx) for i in range(nx)]
    to_left = [(i, (i - 1) % nx) for i in range(nx)]

    group_of = expert_ids // EXP_GROUP
    local_of = expert_ids % EXP_GROUP
    group_hit = (
        group_of[:, :, None] == jnp.arange(groups, dtype=jnp.int32)[None, None, :]
    ).astype(jnp.float32)
    local_hit = (
        local_of[:, :, None] == jnp.arange(EXP_GROUP, dtype=jnp.int32)[None, None, :]
    ).astype(jnp.float32)
    chosen = (jnp.sum(group_hit, axis=1) > 0).astype(jnp.bfloat16)
    send_rows = jnp.einsum(
        "tg,td->gd", chosen, tokens, preferred_element_type=jnp.float32
    ).astype(jnp.bfloat16)
    weighted_hit = local_hit * gates.astype(jnp.float32)[:, :, None]
    gate_table = jnp.sum(
        group_hit[:, :, :, None] * weighted_hit[:, :, None, :], axis=(0, 1)
    ).astype(jnp.bfloat16)
    packed = jnp.concatenate(
        [
            send_rows[:, :FRONT],
            jnp.pad(gate_table, ((0, 0), (0, LANES - EXP_GROUP))),
            send_rows[:, FRONT:],
        ],
        axis=1,
    )
    arrived = lax.all_to_all(packed, "group", split_axis=0, concat_axis=0, tiled=True)
    front = arrived[:, : FRONT + LANES]
    back = arrived[:, FRONT + LANES :]
    back_width = features - FRONT
    half = back_width // 2

    back_own = lax.all_gather(back, "z", axis=0, tiled=True)
    front_x = lax.all_gather(front, "x", axis=0, tiled=True)
    front_all = lax.all_gather(front_x, "z", axis=0, tiled=True)
    back_left = lax.ppermute(back_own, "x", to_right)
    back_right = lax.ppermute(back_own, "x", to_left)
    far_low = lax.ppermute(back_left[:, :half], "x", to_right)
    far_high = lax.ppermute(back_right[:, half:], "x", to_left)

    both = jnp.concatenate([gate_weight[0], up_weight[0]], axis=1)
    both_front, both_back = both[:FRONT], both[FRONT:]

    def dot(a, b):
        return jnp.dot(a, b, preferred_element_type=jnp.float32)

    rows_z = back_own.shape[0]
    by_offset = jnp.stack(
        [
            dot(back_own, both_back),
            dot(back_right, both_back),
            dot(far_low, both_back[:half]) + dot(far_high, both_back[half:]),
            dot(back_left, both_back),
        ]
    ).reshape(nx, nz, groups, 2 * units)
    act_back = jnp.stack(
        [
            lax.dynamic_index_in_dim(by_offset, (x - x_me + nx) % nx, 0, keepdims=False)
            for x in range(nx)
        ],
        axis=1,
    ).reshape(nz * nx * groups, 2 * units)
    act = dot(front_all[:, :FRONT], both_front) + act_back
    hidden = (jax.nn.silu(act[:, :units]) * act[:, units:]).astype(jnp.bfloat16)
    mine = (x_me * nz + lax.axis_index("z")) // slices
    own = (jnp.arange(LANES, dtype=jnp.int32) == mine).astype(jnp.float32)
    scale = jnp.sum(front_all[:, FRONT:].astype(jnp.float32) * own[None, :], axis=1, keepdims=True)

    down = down_weight[0]
    front_out = (dot(hidden, down[:, :FRONT]) * scale).astype(jnp.bfloat16)
    front_z = lax.psum_scatter(front_out, "z", scatter_dimension=0, tiled=True)
    front_parts = lax.all_to_all(front_z, "x", split_axis=0, concat_axis=0, tiled=True)
    front_sum = jnp.sum(
        front_parts.reshape(nx, groups, FRONT), axis=0, dtype=jnp.float32
    ).astype(jnp.bfloat16)

    down_low, down_high = down[:, FRONT : FRONT + half], down[:, FRONT + half :]
    hidden_x = hidden.reshape(nz, nx, groups, units)
    scale_x = scale.reshape(nz, nx, groups, 1)

    def block(offset):
        at = (x_me + offset) % nx
        return (
            lax.dynamic_index_in_dim(hidden_x, at, 1, keepdims=False).reshape(rows_z, units),
            lax.dynamic_index_in_dim(scale_x, at, 1, keepdims=False).reshape(rows_z, 1),
        )

    h_far, s_far = block(2)
    h_right, s_right = block(1)
    h_left, s_left = block(3)
    h_own, s_own = block(0)
    low_in = lax.ppermute((dot(h_far, down_low) * s_far).astype(jnp.bfloat16), "x", to_right)
    high_in = lax.ppermute((dot(h_far, down_high) * s_far).astype(jnp.bfloat16), "x", to_left)
    send_right = jnp.concatenate(
        [dot(h_right, down_low) * s_right + low_in, dot(h_right, down_high) * s_right], axis=1
    ).astype(jnp.bfloat16)
    send_left = jnp.concatenate(
        [dot(h_left, down_low) * s_left, dot(h_left, down_high) * s_left + high_in], axis=1
    ).astype(jnp.bfloat16)
    from_left = lax.ppermute(send_right, "x", to_right)
    from_right = lax.ppermute(send_left, "x", to_left)
    back_out = (dot(h_own, down[:, FRONT:]) * s_own + from_left + from_right).astype(jnp.bfloat16)
    back_sum = lax.psum_scatter(back_out, "z", scatter_dimension=0, tiled=True)

    home = lax.all_to_all(
        jnp.concatenate([front_sum, back_sum], axis=1),
        "group",
        split_axis=0,
        concat_axis=0,
        tiled=True,
    )
    result = jnp.einsum("tg,gd->td", chosen, home, preferred_element_type=jnp.float32)
    return result.astype(jnp.bfloat16)


def solution(mesh):
    groups, columns = mesh.devices.shape
    fine = Mesh(
        mesh.devices.reshape(groups, X_CHIPS, columns // X_CHIPS), ("group", "x", "z")
    )
    lead = ("group", "x", "z")
    in_specs = (
        P(lead, None),
        P(lead, None),
        P(lead, None),
        P(lead, None, None),
        P(lead, None, None),
        P(lead, None, None),
    )
    return jax.shard_map(
        on_device, mesh=fine, in_specs=in_specs, out_specs=P(lead, None), check_vma=False
    )
```

time: 492 us -> 378 us (0.77)
  blocking collectives: 237 us -> 73 us
  waiting for transfers between devices: 194 us -> 233 us
  between operations: 0.16 us -> 13.6 us
    all_to_all x3 -> x0, waiting for transfers between devices: 194 us -> none  [the longest x1 182 us: on_device(): lax.all_to_all(partial_rows.reshape(received.shape), 'expert', split_axis...]
    all_to_all x2 -> x3, blocking collectives: 237 us -> 62.4 us  [the longest x1 27.1 us: on_device(): lax.all_to_all(jnp.concatenate([front_sum, back_sum], axis=1), 'group', s...]
    reduce_scatter x0 -> x2, waiting for transfers between devices: none -> 103 us  [the longest x1 65.1 us: on_device(): back_sum = lax.psum_scatter(back_out, 'z', scatter_dimension=0, tiled=True)]
    all_gather x0 -> x2, waiting for transfers between devices: none -> 92.2 us  [the longest x1 49.1 us: on_device(): back_own = lax.all_gather(back, 'z', axis=0, tiled=True)]
    ppermute x0 -> x8, waiting for transfers between devices: none -> 37.3 us  [the longest x1 10.7 us: on_device(): from_left = lax.ppermute(send_right, 'x', to_right)]
    all_to_all x3 -> x0, starting transfers between devices: 30.2 us -> none  [the longest x1 17.4 us: on_device(): lax.all_to_all(gate_table, 'group', split_axis=0, concat_axis=0, tiled=True)]
    ppermute x0 -> x8, starting transfers between devices: none -> 26.3 us  [the longest x1 5.21 us: on_device(): far_high = lax.ppermute(back_right[:, half:], 'x', to_left)]
    all_gather x0 -> x1, blocking collectives: none -> 10.7 us  [on_device(): front_x = lax.all_gather(front, 'x', axis=0, tiled=True)]
  transfers between devices with their start and end apart: 3 -> 12, of which waited for: 3 -> 10; matrix products, arithmetic and copies ran while one was open for 1% -> 4% of each run, Pallas kernels for 0% -> 0%
where the time goes in v1:
time: 378 us; the launch traced here: 377 us
  waiting for transfers between devices  233 us (62%)
  blocking collectives  73 us (19%)
  starting transfers between devices  26.4 us (7%)
  matrix products  16 us (4%)
  between operations  13.6 us (4%)
  other arithmetic  10.3 us (3%)
  local copies, waits for them, and re-layouts  4.57 us (1%)
    reduce_scatter x1, waiting for transfers between devices, on_device(): back_sum = lax.psum_scatter(back_out, 'z', scatter_dimension=0, tiled=True)  65.1 us
    all_gather x1, waiting for transfers between devices, on_device(): back_own = lax.all_gather(back, 'z', axis=0, tiled=True)  49.1 us
    all_gather x1, waiting for transfers between devices, on_device(): front_all = lax.all_gather(front_x, 'z', axis=0, tiled=True)  43.1 us
    reduce_scatter x1, waiting for transfers between devices, on_device(): front_z = lax.psum_scatter(front_out, 'z', scatter_dimension=0, tiled=True)  38.4 us
    all_to_all x1, blocking collectives, on_device(): lax.all_to_all(jnp.concatenate([front_sum, back_sum], axis=1), 'group', s...  27.1 us
    all_to_all x1, blocking collectives, on_device(): lax.all_to_all(packed, 'group', split_axis=0, concat_axis=0, tiled=True)  25.9 us
    dot_general x14, matrix products, dot(): return jnp.dot(a, b, preferred_element_type=jnp.float32)  14.9 us
    ppermute x1, waiting for transfers between devices, on_device(): from_left = lax.ppermute(send_right, 'x', to_right)  10.7 us
  transfers between devices with their start and end apart: 12, of which 10 were waited for; matrix products, arithmetic and copies ran while one was open for 4% of the time, Pallas kernels for 0%

profile of v1, /device:TPU:1, one launch (start us, length us, event | category | flops | bytes accessed | tf_op | source)
XLA Modules:
  0.0 377.0 jit_solution(15376881608944748114)
XLA Ops:
  10.1 25.9 %all_to_all.33 = bf16[16,2,2112]{2,1,0:T(2,128)(2,1)S(1)} all-to-all(bf16[16,2,2112]{2,1,0:T(2,128)(2,1)S(1)} %reshape.100), channel_id=1, replica_groups=mesh['group'=16,'x'=4,'z'=16] {'group'}, dimensions={0} | all-to-all | bytes 270336 | tf_op jit(solution)/shard_map/all_to_all | solution.py:47
  37.0 10.7 %all_gather.9 = bf16[64,2176]{1,0:T(8,128)(2,1)} all-gather(bf16[16,2176]{1,0:T(8,128)(2,1)S(1)} %slice.76), channel_id=1, replica_groups=mesh['group'=16,'x'=4,'z'=16] {'x'}, dimensions={0}, use_global_device_ids=true | all-gather | bytes 348160 | tf_op jit(solution)/shard_map/all_gather | solution.py:54
  47.7 49.1 %all-gather.5.cloned.1.call-done = bf16[256,2048]{1,0:T(8,128)(2,1)} async-done(((bf16[16,2048]{1,0:T(8,128)(2,1)}), bf16[256,2048]{1,0:T(8,128)(2,1)}) %all-gather.5.cloned.1.call-update) | async-done | bytes 1048592 | tf_op jit(solution)/shard_map/all_gather | solution.py:53
  96.8 4.3 %collective-permute-start = (bf16[256,2048]{1,0:T(8,128)(2,1)}, bf16[256,2048]{1,0:T(8,128)(2,1)S(1)}, u32[]{:S(2)}, u32[]{:S(2)}) collective-permute-start(bf16[256,2048]{1,0:T(8,128)(2,1)} %all-gather.5.cloned.1.call-done), channel_id=1, source_target_pairs={{0,48},{16,0},{32,16},{48,32},{1,49},{17,1},{33,17},{49,33},{2,50}... | collective-permute-start | bytes 3145736 | tf_op jit(solution)/shard_map/ppermute | solution.py:57
  101.1 1.9 collective-permute-start.1
  104.8 9.0 %collective-permute-done = bf16[256,2048]{1,0:T(8,128)(2,1)S(1)} collective-permute-done((bf16[256,2048]{1,0:T(8,128)(2,1)}, bf16[256,2048]{1,0:T(8,128)(2,1)S(1)}, u32[]{:S(2)}, u32[]{:S(2)}) %collective-permute-start) | collective-permute-done | bytes 1048608 | tf_op jit(solution)/shard_map/ppermute | solution.py:57
  113.8 5.2 %collective-permute-start.3 = (bf16[256,1024]{1,0:T(8,128)(2,1)S(1)}, bf16[256,1024]{1,0:T(8,128)(2,1)S(1)}, u32[]{:S(2)}, u32[]{:S(2)}) collective-permute-start(bf16[256,1024]{1,0:T(8,128)(2,1)S(1)} %slice.86), channel_id=1, source_target_pairs={{0,48},{16,0},{32,16},{48,32},{1,49},{17,1},{33,17},{49,33},{2,50}... | collective-permute-start | bytes 1572872 | tf_op jit(solution)/shard_map/ppermute | solution.py:59
  120.1 1.9 collective-permute-start.2
  124.1 5.8 %collective-permute-done.3 = bf16[256,1024]{1,0:T(8,128)(2,1)S(1)} collective-permute-done((bf16[256,1024]{1,0:T(8,128)(2,1)S(1)}, bf16[256,1024]{1,0:T(8,128)(2,1)S(1)}, u32[]{:S(2)}, u32[]{:S(2)}) %collective-permute-start.3) | collective-permute-done | bytes 524320 | tf_op jit(solution)/shard_map/ppermute | solution.py:59
  130.2 5.1 %collective-permute-done.2 = bf16[256,1024]{1,0:T(8,128)(2,1)S(1)} collective-permute-done((bf16[256,1024]{1,0:T(8,128)(2,1)S(1)}, bf16[256,1024]{1,0:T(8,128)(2,1)S(1)}, u32[]{:S(2)}, u32[]{:S(2)}) %collective-permute-start.2) | collective-permute-done | bytes 524320 | tf_op jit(solution)/shard_map/ppermute | solution.py:58
  136.9 43.1 %all-gather.3.cloned.1.call-done = bf16[1024,2176]{1,0:T(8,128)(2,1)} async-done(((bf16[64,2176]{1,0:T(8,128)(2,1)}), bf16[1024,2176]{1,0:T(8,128)(2,1)}) %all-gather.3.cloned.1.call-update) | async-done | bytes 4456464 | tf_op jit(solution)/shard_map/all_gather | solution.py:55
  180.0 3.8 %fusion.2 = f32[1024,256]{1,0:T(8,128)S(1)} fusion(f32[1024,256]{1,0:T(8,128)} %bitcast.68, bf16[1024,2176]{1,0:T(8,128)(2,1)} %all-gather.3.cloned.1.call-done, bf16[4096,128]{1,0:T(8,128)(2,1)S(1)} %bitcast.54, bf16[4096,128]{1,0:T(8,128)(2,1)S(1)} %bitcast.58), kind=kOutput, calls=%fused_computation.19 | convolution fusion | flops 1076101120 | bytes 8388608 | tf_op jit(solution)/shard_map/dot_general | solution.py:65
  185.1 3.2 multiply_convert_fusion
  189.8 3.4 collective-permute-start.4
  194.5 3.1 collective-permute-start.6
  198.1 3.1 collective-permute-done.4
  203.7 2.2 collective-permute-start.5
  207.3 4.3 %collective-permute-start.7 = (bf16[256,2048]{1,0:T(8,128)(2,1)}, bf16[256,2048]{1,0:T(8,128)(2,1)S(1)}, u32[]{:S(2)}, u32[]{:S(2)}) collective-permute-start(bf16[256,2048]{1,0:T(8,128)(2,1)} %pad_maximum_fusion.3), channel_id=1, source_target_pairs={{0,48},{16,0},{32,16},{48,32},{1,49},{17,1},{33,17},{49,33},{2,50}... | collective-permute-start | bytes 3145736 | tf_op jit(solution)/shard_map/ppermute | solution.py:121
  212.1 10.7 %collective-permute-done.5 = bf16[256,2048]{1,0:T(8,128)(2,1)S(1)} collective-permute-done((bf16[256,2048]{1,0:T(8,128)(2,1)}, bf16[256,2048]{1,0:T(8,128)(2,1)S(1)}, u32[]{:S(2)}, u32[]{:S(2)}) %collective-permute-start.5) | collective-permute-done | bytes 1048608 | tf_op jit(solution)/shard_map/ppermute | solution.py:120
  222.8 3.6 collective-permute-done.7
  227.9 38.4 %reduce-scatter.3.cloned.1.call-done = bf16[64,2048]{1,0:T(8,128)(2,1)} async-done(((bf16[1024,2048]{1,0:T(8,128)(2,1)}), bf16[64,2048]{1,0:T(8,128)(2,1)}) %reduce-scatter.3.cloned.1.call-update) | async-done | bytes 262160 | tf_op jit(solution)/shard_map/reduce_scatter | solution.py:91
  266.3 9.3 %all_to_all.34 = bf16[4,16,2048]{2,1,0:T(8,128)(2,1)S(1)} all-to-all(bf16[4,16,2048]{2,1,0:T(8,128)(2,1)} %bitcast.81), channel_id=1, replica_groups=mesh['group'=16,'x'=4,'z'=16] {'x'}, dimensions={0} | all-to-all | bytes 524288 | tf_op jit(solution)/shard_map/all_to_all | solution.py:92
  275.7 65.1 %reduce-scatter.5.cloned.1.call-done = bf16[16,2048]{1,0:T(8,128)(2,1)} async-done(((bf16[256,2048]{1,0:T(8,128)(2,1)}), bf16[16,2048]{1,0:T(8,128)(2,1)}) %reduce-scatter.5.cloned.1.call-update) | async-done | bytes 65552 | tf_op jit(solution)/shard_map/reduce_scatter | solution.py:123
  342.4 27.1 %all_to_all.35 = bf16[16,2,2048]{2,1,0:T(2,128)(2,1)S(1)} all-to-all(bf16[16,2,2048]{2,1,0:T(2,128)(2,1)S(1)} %reshape.102), channel_id=1, replica_groups=mesh['group'=16,'x'=4,'z'=16] {'group'}, dimensions={0} | all-to-all | bytes 262144 | tf_op jit(solution)/shard_map/all_to_all | solution.py:125
  (74 shorter events, 24.1 us)
Async XLA Ops:
  6.5 1.0 copy-start
  6.5 96.6 %copy-start.1 = (bf16[1,4096,128]{2,1,0:T(8,128)(2,1)S(1)}, bf16[1,4096,128]{2,1,0:T(8,128)(2,1)}, u32[]{:S(2)}) copy-start(bf16[1,4096,128]{2,1,0:T(8,128)(2,1)} %param.9) | copy-start | bytes 3145732
  6.5 96.6 %copy-start.2 = (bf16[1,4096,128]{2,1,0:T(8,128)(2,1)S(1)}, bf16[1,4096,128]{2,1,0:T(8,128)(2,1)}, u32[]{:S(2)}) copy-start(bf16[1,4096,128]{2,1,0:T(8,128)(2,1)} %param.10) | copy-start | bytes 3145732
  6.5 90.3 %all-gather.5.cloned.1.call-start = ((), (), s32[]{:S(2)}) async-start(), calls=%async_computation.6 | async-start | bytes 1114112 | tf_op jit(solution)/shard_map/all_gather | solution.py:53
  36.9 143.1 %all-gather.3.cloned.1.call-start = ((), (), s32[]{:S(2)}) async-start(), calls=%async_computation.5 | async-start | bytes 4734976 | tf_op jit(solution)/shard_map/all_gather | solution.py:55
  47.7 218.7 %reduce-scatter.3.cloned.1.call-start = ((), (), s32[]{:S(2)}) async-start(), calls=%async_computation.7 | async-start | bytes 4456448 | tf_op jit(solution)/shard_map/reduce_scatter | solution.py:91
  96.8 16.9 %collective-permute-start = (bf16[256,2048]{1,0:T(8,128)(2,1)}, bf16[256,2048]{1,0:T(8,128)(2,1)S(1)}, u32[]{:S(2)}, u32[]{:S(2)}) collective-permute-start(bf16[256,2048]{1,0:T(8,128)(2,1)} %all-gather.5.cloned.1.call-done), channel_id=1, source_target_pairs={{0,48},{16,0},{32,16},{48,32},{1,49},{17,1},{33,17},{49,33},{2,50}... | collective-permute-start | bytes 3145736 | tf_op jit(solution)/shard_map/ppermute | solution.py:57
  101.1 17.9 %collective-permute-start.1 = (bf16[256,2048]{1,0:T(8,128)(2,1)}, bf16[256,2048]{1,0:T(8,128)(2,1)}, u32[]{:S(2)}, u32[]{:S(2)}) collective-permute-start(bf16[256,2048]{1,0:T(8,128)(2,1)} %all-gather.5.cloned.1.call-done), channel_id=1, source_target_pairs={{0,16},{16,32},{32,48},{48,0},{1,17},{17,33},{33,49},{49,1},{2,18}... | collective-permute-start | bytes 3145736 | tf_op jit(solution)/shard_map/ppermute | solution.py:56
  103.1 1.2 copy-start.4
  113.8 16.1 %collective-permute-start.3 = (bf16[256,1024]{1,0:T(8,128)(2,1)S(1)}, bf16[256,1024]{1,0:T(8,128)(2,1)S(1)}, u32[]{:S(2)}, u32[]{:S(2)}) collective-permute-start(bf16[256,1024]{1,0:T(8,128)(2,1)S(1)} %slice.86), channel_id=1, source_target_pairs={{0,48},{16,0},{32,16},{48,32},{1,49},{17,1},{33,17},{49,33},{2,50}... | collective-permute-start | bytes 1572872 | tf_op jit(solution)/shard_map/ppermute | solution.py:59
  120.1 15.2 %collective-permute-start.2 = (bf16[256,1024]{1,0:T(8,128)(2,1)S(1)}, bf16[256,1024]{1,0:T(8,128)(2,1)S(1)}, u32[]{:S(2)}, u32[]{:S(2)}) collective-permute-start(bf16[256,1024]{1,0:T(8,128)(2,1)S(1)} %slice.83), channel_id=1, source_target_pairs={{0,16},{16,32},{32,48},{48,0},{1,17},{17,33},{33,49},{49,1},{2,18}... | collective-permute-start | bytes 1572872 | tf_op jit(solution)/shard_map/ppermute | solution.py:58
  180.0 5.1 %copy-start.3 = (bf16[1,128,4096]{2,1,0:T(8,128)(2,1)S(1)}, bf16[1,128,4096]{2,1,0:T(8,128)(2,1)}, u32[]{:S(2)}) copy-start(bf16[1,128,4096]{2,1,0:T(8,128)(2,1)} %param.11) | copy-start | bytes 3145732
  188.3 152.5 %reduce-scatter.5.cloned.1.call-start = ((), (), s32[]{:S(2)}) async-start(), calls=%async_computation.8 | async-start | bytes 1114112 | tf_op jit(solution)/shard_map/reduce_scatter | solution.py:123
  189.8 11.4 %collective-permute-start.4 = (bf16[256,1024]{1,0:T(8,128)(2,1)}, bf16[256,1024]{1,0:T(8,128)(2,1)}, u32[]{:S(2)}, u32[]{:S(2)}) collective-permute-start(bf16[256,1024]{1,0:T(8,128)(2,1)} %fusion.5), channel_id=1, source_target_pairs={{0,16},{16,32},{32,48},{48,0},{1,17},{17,33},{33,49},{49,1},{2,18}... | collective-permute-start | bytes 1572872 | tf_op jit(solution)/shard_map/ppermute | solution.py:112
  194.5 11.4 %collective-permute-start.6 = (bf16[256,1024]{1,0:T(8,128)(2,1)}, bf16[256,1024]{1,0:T(8,128)(2,1)S(1)}, u32[]{:S(2)}, u32[]{:S(2)}) collective-permute-start(bf16[256,1024]{1,0:T(8,128)(2,1)} %fusion.8), channel_id=1, source_target_pairs={{0,48},{16,0},{32,16},{48,32},{1,49},{17,1},{33,17},{49,33},{2,50}... | collective-permute-start | bytes 1572872 | tf_op jit(solution)/shard_map/ppermute | solution.py:113
  203.7 19.1 %collective-permute-start.5 = (bf16[256,2048]{1,0:T(8,128)(2,1)}, bf16[256,2048]{1,0:T(8,128)(2,1)S(1)}, u32[]{:S(2)}, u32[]{:S(2)}) collective-permute-start(bf16[256,2048]{1,0:T(8,128)(2,1)} %pad_maximum_fusion.2), channel_id=1, source_target_pairs={{0,16},{16,32},{32,48},{48,0},{1,17},{17,33},{33,49},{49,1},{2,18}... | collective-permute-start | bytes 3145736 | tf_op jit(solution)/shard_map/ppermute | solution.py:120
  207.3 19.1 %collective-permute-start.7 = (bf16[256,2048]{1,0:T(8,128)(2,1)}, bf16[256,2048]{1,0:T(8,128)(2,1)S(1)}, u32[]{:S(2)}, u32[]{:S(2)}) collective-permute-start(bf16[256,2048]{1,0:T(8,128)(2,1)} %pad_maximum_fusion.3), channel_id=1, source_target_pairs={{0,48},{16,0},{32,16},{48,32},{1,49},{17,1},{33,17},{49,33},{2,50}... | collective-permute-start | bytes 3145736 | tf_op jit(solution)/shard_map/ppermute | solution.py:121
Sparse Core Ops, SparseCore 0:
  37.0 59.7 all-gather.4
  99.5 80.4 all-gather.2
  188.4 77.8 reduce-scatter.2
  269.6 71.1 reduce-scatter.4

commit v2 on v1

--- a/solution.py
+++ b/solution.py
@@ -6,7 +6,7 @@
 EXP_GROUP = 8
 LANES = 128
 X_CHIPS = 4
-FRONT = 2048
+FRONT = 3072
 
 
 def on_device(tokens, expert_ids, gates, gate_weight, up_weight, down_weight):
@@ -36,23 +36,25 @@
     gate_table = jnp.sum(
         group_hit[:, :, :, None] * weighted_hit[:, :, None, :], axis=(0, 1)
     ).astype(jnp.bfloat16)
-    packed = jnp.concatenate(
-        [
-            send_rows[:, :FRONT],
-            jnp.pad(gate_table, ((0, 0), (0, LANES - EXP_GROUP))),
-            send_rows[:, FRONT:],
-        ],
-        axis=1,
+    width = features - FRONT
+    half = width // 2
+    front_row = jnp.concatenate(
+        [send_rows[:, :FRONT], jnp.pad(gate_table, ((0, 0), (0, LANES - EXP_GROUP)))], axis=1
     )
-    arrived = lax.all_to_all(packed, "group", split_axis=0, concat_axis=0, tiled=True)
-    front = arrived[:, : FRONT + LANES]
-    back = arrived[:, FRONT + LANES :]
-    back_width = features - FRONT
-    half = back_width // 2
 
+    front = lax.all_to_all(
+        jnp.broadcast_to(front_row[:, None], (groups, nx, FRONT + LANES)).reshape(
+            groups * nx, FRONT + LANES
+        ),
+        ("group", "x"),
+        split_axis=0,
+        concat_axis=0,
+        tiled=True,
+    )
+    front_all = lax.all_gather(front, "z", axis=0, tiled=True)
+    back_row, _ = lax.optimization_barrier((send_rows[:, FRONT:], front))
+    back = lax.all_to_all(back_row, "group", split_axis=0, concat_axis=0, tiled=True)
     back_own = lax.all_gather(back, "z", axis=0, tiled=True)
-    front_x = lax.all_gather(front, "x", axis=0, tiled=True)
-    front_all = lax.all_gather(front_x, "z", axis=0, tiled=True)
     back_left = lax.ppermute(back_own, "x", to_right)
     back_right = lax.ppermute(back_own, "x", to_left)
     far_low = lax.ppermute(back_left[:, :half], "x", to_right)
@@ -78,8 +80,8 @@
             lax.dynamic_index_in_dim(by_offset, (x - x_me + nx) % nx, 0, keepdims=False)
             for x in range(nx)
         ],
-        axis=1,
-    ).reshape(nz * nx * groups, 2 * units)
+        axis=2,
+    ).reshape(nz * groups * nx, 2 * units)
     act = dot(front_all[:, :FRONT], both_front) + act_back
     hidden = (jax.nn.silu(act[:, :units]) * act[:, units:]).astype(jnp.bfloat16)
     mine = (x_me * nz + lax.axis_index("z")) // slices
@@ -89,20 +91,15 @@
     down = down_weight[0]
     front_out = (dot(hidden, down[:, :FRONT]) * scale).astype(jnp.bfloat16)
     front_z = lax.psum_scatter(front_out, "z", scatter_dimension=0, tiled=True)
-    front_parts = lax.all_to_all(front_z, "x", split_axis=0, concat_axis=0, tiled=True)
-    front_sum = jnp.sum(
-        front_parts.reshape(nx, groups, FRONT), axis=0, dtype=jnp.float32
-    ).astype(jnp.bfloat16)
-
     down_low, down_high = down[:, FRONT : FRONT + half], down[:, FRONT + half :]
-    hidden_x = hidden.reshape(nz, nx, groups, units)
-    scale_x = scale.reshape(nz, nx, groups, 1)
+    hidden_x = hidden.reshape(nz, groups, nx, units)
+    scale_x = scale.reshape(nz, groups, nx, 1)
 
     def block(offset):
         at = (x_me + offset) % nx
         return (
-            lax.dynamic_index_in_dim(hidden_x, at, 1, keepdims=False).reshape(rows_z, units),
-            lax.dynamic_index_in_dim(scale_x, at, 1, keepdims=False).reshape(rows_z, 1),
+            lax.dynamic_index_in_dim(hidden_x, at, 2, keepdims=False).reshape(rows_z, units),
+            lax.dynamic_index_in_dim(scale_x, at, 2, keepdims=False).reshape(rows_z, 1),
         )
 
     h_far, s_far = block(2)
@@ -120,16 +117,17 @@
     from_left = lax.ppermute(send_right, "x", to_right)
     from_right = lax.ppermute(send_left, "x", to_left)
     back_out = (dot(h_own, down[:, FRONT:]) * s_own + from_left + from_right).astype(jnp.bfloat16)
-    back_sum = lax.psum_scatter(back_out, "z", scatter_dimension=0, tiled=True)
-
-    home = lax.all_to_all(
-        jnp.concatenate([front_sum, back_sum], axis=1),
-        "group",
-        split_axis=0,
-        concat_axis=0,
-        tiled=True,
+    back_parts = lax.all_to_all(back_out, "z", split_axis=0, concat_axis=0, tiled=True)
+    back_sum = jnp.sum(
+        back_parts.reshape(nz, groups, width), axis=0, dtype=jnp.float32
+    ).astype(jnp.bfloat16)
+    back_home = lax.all_to_all(back_sum, "group", split_axis=0, concat_axis=0, tiled=True)
+    front_home = lax.all_to_all(
+        front_z, ("group", "x"), split_axis=0, concat_axis=0, tiled=True
     )
-    result = jnp.einsum("tg,gd->td", chosen, home, preferred_element_type=jnp.float32)
+    result = jnp.concatenate(
+        [dot(jnp.repeat(chosen, nx, axis=1), front_home), dot(chosen, back_home)], axis=1
+    )
     return result.astype(jnp.bfloat16)
 
 

time: 378 us -> 299 us (0.79)
  waiting for transfers between devices: 233 us -> 74.8 us
  blocking collectives: 73 us -> 121 us
  starting transfers between devices: 26.4 us -> 52.8 us
  local copies, waits for them, and re-layouts: 4.57 us -> 9.76 us
    all_gather x2 -> x1, waiting for transfers between devices: 92.2 us -> 14.5 us  [on_device(): front_all = lax.all_gather(front, 'z', axis=0, tiled=True)]
    reduce_scatter x1 -> x0, waiting for transfers between devices: 65.1 us -> none  [on_device(): back_sum = lax.psum_scatter(back_out, 'z', scatter_dimension=0, tiled=True)]
    all_to_all x0 -> x2, starting transfers between devices: none -> 28.7 us  [the longest x1 15.3 us: on_device(): lax.all_to_all(front_z, ('group', 'x'), split_axis=0, concat_axis=0, tile...]
    all_gather x1, blocking collectives: 10.7 us -> 39.3 us  [on_device(): back_own = lax.all_gather(back, 'z', axis=0, tiled=True)]
    all_to_all x3, blocking collectives: 62.4 us -> 81.7 us  [the longest x1 36.8 us: on_device(): lax.all_to_all(back_out, 'z', split_axis=0, concat_axis=0, tiled=True)]
    all_to_all x0 -> x2, waiting for transfers between devices: none -> 14.3 us  [the longest x1 14.3 us: on_device(): lax.all_to_all(front_z, ('group', 'x'), split_axis=0, concat_axis=0, tile...]
    reduce_scatter x1, waiting for transfers between devices: 38.4 us -> 24.6 us  [on_device(): front_z = lax.psum_scatter(front_out, 'z', scatter_dimension=0, tiled=True)]
    ppermute x1, waiting for transfers between devices: 5.77 us -> 0.01 us  [on_device(): far_high = lax.ppermute(back_right[:, half:], 'x', to_left)]
  transfers between devices with their start and end apart: 12 -> 12, of which waited for: 10 -> 8; matrix products, arithmetic and copies ran while one was open for 4% -> 5% of each run, Pallas kernels for 0% -> 0%
where the time goes in v2:
time: 299 us; the launch traced here: 298 us
  blocking collectives  121 us (40%)
  waiting for transfers between devices  74.8 us (25%)
  starting transfers between devices  52.8 us (18%)
  between operations  14.1 us (5%)
  matrix products  14 us (5%)
  other arithmetic  11.7 us (4%)
  local copies, waits for them, and re-layouts  9.76 us (3%)
    all_gather x1, blocking collectives, on_device(): back_own = lax.all_gather(back, 'z', axis=0, tiled=True)  39.3 us
    all_to_all x1, blocking collectives, on_device(): lax.all_to_all(back_out, 'z', split_axis=0, concat_axis=0, tiled=True)  36.8 us
    all_to_all x1, blocking collectives, on_device(): lax.all_to_all(jnp.broadcast_to(front_row[:, None], (groups, nx, FRONT +...  33 us
    reduce_scatter x1, waiting for transfers between devices, on_device(): front_z = lax.psum_scatter(front_out, 'z', scatter_dimension=0, tiled=True)  24.6 us
    all_to_all x1, starting transfers between devices, on_device(): lax.all_to_all(front_z, ('group', 'x'), split_axis=0, concat_axis=0, tile...  15.3 us
    all_gather x1, waiting for transfers between devices, on_device(): front_all = lax.all_gather(front, 'z', axis=0, tiled=True)  14.5 us
    all_to_all x1, waiting for transfers between devices, on_device(): lax.all_to_all(front_z, ('group', 'x'), split_axis=0, concat_axis=0, tile...  14.3 us
    dot_general x16, matrix products, dot(): return jnp.dot(a, b, preferred_element_type=jnp.float32)  13.7 us
  transfers between devices with their start and end apart: 12, of which 8 were waited for; matrix products, arithmetic and copies ran while one was open for 5% of the time, Pallas kernels for 0%

profile of v2, /device:TPU:1, one launch (start us, length us, event | category | flops | bytes accessed | tf_op | source)
XLA Modules:
  0.0 297.9 jit_solution(3866065834301289435)
XLA Ops:
  9.6 3.1 %reduce.11 = bf16[64,3200]{1,0:T(8,128)(2,1)S(1)} reduce(bf16[64,1,3200]{2,1,0:T(2,128)(2,1)S(1)} %all_to_all.52, bf16[]{:T(256)} %broadcast.81), dimensions={1}, to_apply=%all_to_all.52.reduce_sub_computation | reduce | bytes 819202 | tf_op jit(solution)/shard_map/all_to_all | solution.py:45
  13.2 33.0 %all_to_all.58 = bf16[64,2,1600]{2,1,0:T(2,128)(2,1)S(1)} all-to-all(bf16[64,2,1600]{2,1,0:T(2,128)(2,1)S(1)} %reshape.97), channel_id=1, replica_groups=mesh['group'=16,'x'=4,'z'=16] {'group','x'}, dimensions={0} | all-to-all | bytes 819200 | tf_op jit(solution)/shard_map/all_to_all | solution.py:45
  48.4 11.9 %all_to_all.59 = bf16[16,2,512]{2,1,0:T(2,128)(2,1)S(1)} all-to-all(bf16[16,2,512]{2,1,0:T(2,128)(2,1)S(1)} %reshape.95), channel_id=1, replica_groups=mesh['group'=16,'x'=4,'z'=16] {'group'}, dimensions={0} | all-to-all | bytes 65536 | tf_op jit(solution)/shard_map/all_to_all | solution.py:56
  60.3 39.3 %all-gather.1 = bf16[256,1,1024]{2,0,1:T(8,128)(2,1)S(1)} all-gather(bf16[16,1,1024]{2,0,1:T(8,128)(2,1)S(1)} %copy.42), channel_id=3, replica_groups=mesh['group'=16,'x'=4,'z'=16] {'z'}, dimensions={0}, use_global_device_ids=true | all-gather | bytes 557056 | tf_op jit(solution)/shard_map/all_gather | solution.py:57
  99.6 2.4 collective-permute-start
  102.0 2.9 collective-permute-start.1
  105.4 5.6 %collective-permute-done = bf16[256,1024]{1,0:T(8,128)(2,1)S(1)} collective-permute-done((bf16[256,1024]{1,0:T(8,128)(2,1)S(1)}, bf16[256,1024]{1,0:T(8,128)(2,1)S(1)}, u32[]{:S(2)}, u32[]{:S(2)}) %collective-permute-start) | collective-permute-done | bytes 524320 | tf_op jit(solution)/shard_map/ppermute | solution.py:59
  111.0 2.8 collective-permute-start.3
  114.8 2.7 collective-permute-start.2
  119.4 4.1 %collective-permute-done.2 = bf16[256,512]{1,0:T(8,128)(2,1)S(1)} collective-permute-done((bf16[256,512]{1,0:T(8,128)(2,1)S(1)}, bf16[256,512]{1,0:T(8,128)(2,1)S(1)}, u32[]{:S(2)}, u32[]{:S(2)}) %collective-permute-start.2) | collective-permute-done | bytes 262176 | tf_op jit(solution)/shard_map/ppermute | solution.py:60
  127.1 14.5 %all-gather.4.cloned.1.call-done = bf16[1024,1,3200]{2,0,1:T(8,128)(2,1)} async-done(((bf16[64,1,3200]{2,0,1:T(8,128)(2,1)}), bf16[1024,1,3200]{2,0,1:T(8,128)(2,1)}) %all-gather.4.cloned.1.call-update) | async-done | bytes 6553616 | tf_op jit(solution)/shard_map/all_gather | solution.py:54
  141.6 4.9 %fusion.4 = f32[1024,256]{1,0:T(8,128)S(1)} fusion(f32[1024,256]{1,0:T(8,128)} %reshape.83, bf16[4096,128]{1,0:T(8,128)(2,1)S(1)} %bitcast.56, bf16[4096,128]{1,0:T(8,128)(2,1)S(1)} %bitcast.60, bf16[1024,3200]{1,0:T(8,128)(2,1)} %bitcast.87), kind=kOutput, calls=%fused_computation.13 | convolution fusion | flops 1614020608 | bytes 10485760 | tf_op jit(solution)/shard_map/dot_general | solution.py:67
  147.8 4.5 %multiply_convert_fusion = bf16[1024,3072]{1,0:T(8,128)(2,1)} fusion(bf16[1024,128]{1,0:T(8,128)(2,1)S(1)} %get-tuple-element.23, f32[1024]{0:T(1024)S(1)} %get-tuple-element.24, bf16[128,4096]{1,0:T(8,128)(2,1)S(1)} %bitcast.62), kind=kOutput, calls=%fused_computation | convolution fusion | flops 811597824 | bytes 7344128 | tf_op jit(solution)/shard_map/dot_general | solution.py:67
  153.7 3.1 %collective-permute-start.4 = (bf16[256,512]{1,0:T(8,128)(2,1)S(1)}, bf16[256,512]{1,0:T(8,128)(2,1)S(1)}, u32[]{:S(2)}, u32[]{:S(2)}) collective-permute-start(bf16[256,512]{1,0:T(8,128)(2,1)S(1)} %fusion.9), channel_id=1, source_target_pairs={{0,16},{16,32},{32,48},{48,0},{1,17},{17,33},{33,49},{49,1},{2,18}... | collective-permute-start | bytes 786440 | tf_op jit(solution)/shard_map/ppermute | solution.py:109
  157.2 3.6 %collective-permute-start.6 = (bf16[256,512]{1,0:T(8,128)(2,1)S(1)}, bf16[256,512]{1,0:T(8,128)(2,1)S(1)}, u32[]{:S(2)}, u32[]{:S(2)}) collective-permute-start(bf16[256,512]{1,0:T(8,128)(2,1)S(1)} %fusion.12), channel_id=1, source_target_pairs={{0,48},{16,0},{32,16},{48,32},{1,49},{17,1},{33,17},{49,33},{2,50}... | collective-permute-start | bytes 786440 | tf_op jit(solution)/shard_map/ppermute | solution.py:110
  161.4 2.4 collective-permute-done.4
  164.1 1.9 collective-permute-start.5
  166.3 4.6 %collective-permute-start.7 = (bf16[256,1024]{1,0:T(8,128)(2,1)S(1)}, bf16[256,1024]{1,0:T(8,128)(2,1)S(1)}, u32[]{:S(2)}, u32[]{:S(2)}) collective-permute-start(bf16[256,1024]{1,0:T(8,128)(2,1)S(1)} %pad_maximum_fusion.3), channel_id=1, source_target_pairs={{0,48},{16,0},{32,16},{48,32},{1,49},{17,1},{33,17},{49,33},{2,50}... | collective-permute-start | bytes 1572872 | tf_op jit(solution)/shard_map/ppermute | solution.py:118
  171.3 7.4 %collective-permute-done.5 = bf16[256,1024]{1,0:T(8,128)(2,1)S(1)} collective-permute-done((bf16[256,1024]{1,0:T(8,128)(2,1)S(1)}, bf16[256,1024]{1,0:T(8,128)(2,1)S(1)}, u32[]{:S(2)}, u32[]{:S(2)}) %collective-permute-start.5) | collective-permute-done | bytes 524320 | tf_op jit(solution)/shard_map/ppermute | solution.py:117
  180.7 36.8 %all_to_all.60 = bf16[16,16,1024]{2,1,0:T(8,128)(2,1)S(1)} all-to-all(bf16[16,16,1024]{2,1,0:T(8,128)(2,1)S(1)} %bitcast.70), channel_id=1, replica_groups=mesh['group'=16,'x'=4,'z'=16] {'z'}, dimensions={0} | all-to-all | bytes 1048576 | tf_op jit(solution)/shard_map/all_to_all | solution.py:120
  219.0 13.4 %all-to-all-start.4 = ((bf16[16,2,512]{2,1,0:T(2,128)(2,1)}), bf16[16,2,512]{2,1,0:T(2,128)(2,1)S(1)}, u32[]{:S(2)}, u32[]{:S(2)}) async-start(bf16[16,2,512]{2,1,0:T(2,128)(2,1)} %reshape.99), calls=%async_computation.5 | async-start | bytes 65536 | tf_op jit(solution)/shard_map/all_to_all | solution.py:124
  232.4 24.6 %reduce-scatter.2.cloned.1.call-done = bf16[64,3072]{1,0:T(8,128)(2,1)} async-done(((bf16[1024,3072]{1,0:T(8,128)(2,1)}), bf16[64,3072]{1,0:T(8,128)(2,1)}) %reduce-scatter.2.cloned.1.call-update) | async-done | bytes 393232 | tf_op jit(solution)/shard_map/reduce_scatter | solution.py:93
  259.9 15.3 %all-to-all-start.2 = ((bf16[64,2,1536]{2,1,0:T(2,128)(2,1)}), bf16[64,2,1536]{2,1,0:T(2,128)(2,1)S(1)}, u32[]{:S(2)}, u32[]{:S(2)}) async-start(bf16[64,2,1536]{2,1,0:T(2,128)(2,1)} %reshape.101), calls=%async_computation.3 | async-start | bytes 786432 | tf_op jit(solution)/shard_map/all_to_all | solution.py:125
  275.6 14.3 %all-to-all-done.2 = bf16[64,2,1536]{2,1,0:T(2,128)(2,1)S(1)} async-done(((bf16[64,2,1536]{2,1,0:T(2,128)(2,1)}), bf16[64,2,1536]{2,1,0:T(2,128)(2,1)S(1)}, u32[]{:S(2)}, u32[]{:S(2)}) %all-to-all-start.2) | async-done | bytes 393248 | tf_op jit(solution)/shard_map/all_to_all | solution.py:125
  (90 shorter events, 24.8 us)
Async XLA Ops:
  6.5 0.9 copy-start
  6.5 135.1 %all-gather.4.cloned.1.call-start = ((), (), s32[]{:S(2)}) async-start(), calls=%async_computation.7 | async-start | bytes 6963200 | tf_op jit(solution)/shard_map/all_gather | solution.py:54
  12.7 92.3 %copy-start.1 = (bf16[1,4096,128]{2,1,0:T(8,128)(2,1)S(1)}, bf16[1,4096,128]{2,1,0:T(8,128)(2,1)}, u32[]{:S(2)}) copy-start(bf16[1,4096,128]{2,1,0:T(8,128)(2,1)} %param.9) | copy-start | bytes 3145732
  12.7 92.3 %copy-start.2 = (bf16[1,4096,128]{2,1,0:T(8,128)(2,1)S(1)}, bf16[1,4096,128]{2,1,0:T(8,128)(2,1)}, u32[]{:S(2)}) copy-start(bf16[1,4096,128]{2,1,0:T(8,128)(2,1)} %param.10) | copy-start | bytes 3145732
  47.6 209.4 %reduce-scatter.2.cloned.1.call-start = ((), (), s32[]{:S(2)}) async-start(), calls=%async_computation.6 | async-start | bytes 6684672 | tf_op jit(solution)/shard_map/reduce_scatter | solution.py:93
  99.6 11.4 %collective-permute-start = (bf16[256,1024]{1,0:T(8,128)(2,1)S(1)}, bf16[256,1024]{1,0:T(8,128)(2,1)S(1)}, u32[]{:S(2)}, u32[]{:S(2)}) collective-permute-start(bf16[256,1024]{1,0:T(8,128)(2,1)S(1)} %bitcast.71), channel_id=1, source_target_pairs={{0,48},{16,0},{32,16},{48,32},{1,49},{17,1},{33,17},{49,33},{2,50}... | collective-permute-start | bytes 1572872 | tf_op jit(solution)/shard_map/ppermute | solution.py:59
  102.0 11.8 %collective-permute-start.1 = (bf16[256,1024]{1,0:T(8,128)(2,1)S(1)}, bf16[256,1024]{1,0:T(8,128)(2,1)}, u32[]{:S(2)}, u32[]{:S(2)}) collective-permute-start(bf16[256,1024]{1,0:T(8,128)(2,1)S(1)} %bitcast.72), channel_id=1, source_target_pairs={{0,16},{16,32},{32,48},{48,0},{1,17},{17,33},{33,49},{49,1},{2,18}... | collective-permute-start | bytes 1572872 | tf_op jit(solution)/shard_map/ppermute | solution.py:58
  111.0 8.1 %collective-permute-start.3 = (bf16[256,512]{1,0:T(8,128)(2,1)S(1)}, bf16[256,512]{1,0:T(8,128)(2,1)S(1)}, u32[]{:S(2)}, u32[]{:S(2)}) collective-permute-start(bf16[256,512]{1,0:T(8,128)(2,1)S(1)} %slice.76), channel_id=1, source_target_pairs={{0,48},{16,0},{32,16},{48,32},{1,49},{17,1},{33,17},{49,33},{2,50}... | collective-permute-start | bytes 786440 | tf_op jit(solution)/shard_map/ppermute | solution.py:61
  114.8 8.7 %collective-permute-start.2 = (bf16[256,512]{1,0:T(8,128)(2,1)S(1)}, bf16[256,512]{1,0:T(8,128)(2,1)S(1)}, u32[]{:S(2)}, u32[]{:S(2)}) collective-permute-start(bf16[256,512]{1,0:T(8,128)(2,1)S(1)} %slice.73), channel_id=1, source_target_pairs={{0,16},{16,32},{32,48},{48,0},{1,17},{17,33},{33,49},{49,1},{2,18}... | collective-permute-start | bytes 786440 | tf_op jit(solution)/shard_map/ppermute | solution.py:60
  141.6 6.2 %copy-start.3 = (bf16[1,128,4096]{2,1,0:T(8,128)(2,1)S(1)}, bf16[1,128,4096]{2,1,0:T(8,128)(2,1)}, u32[]{:S(2)}) copy-start(bf16[1,128,4096]{2,1,0:T(8,128)(2,1)} %param.11) | copy-start | bytes 3145732
  153.7 10.0 %collective-permute-start.4 = (bf16[256,512]{1,0:T(8,128)(2,1)S(1)}, bf16[256,512]{1,0:T(8,128)(2,1)S(1)}, u32[]{:S(2)}, u32[]{:S(2)}) collective-permute-start(bf16[256,512]{1,0:T(8,128)(2,1)S(1)} %fusion.9), channel_id=1, source_target_pairs={{0,16},{16,32},{32,48},{48,0},{1,17},{17,33},{33,49},{49,1},{2,18}... | collective-permute-start | bytes 786440 | tf_op jit(solution)/shard_map/ppermute | solution.py:109
  157.2 8.8 %collective-permute-start.6 = (bf16[256,512]{1,0:T(8,128)(2,1)S(1)}, bf16[256,512]{1,0:T(8,128)(2,1)S(1)}, u32[]{:S(2)}, u32[]{:S(2)}) collective-permute-start(bf16[256,512]{1,0:T(8,128)(2,1)S(1)} %fusion.12), channel_id=1, source_target_pairs={{0,48},{16,0},{32,16},{48,32},{1,49},{17,1},{33,17},{49,33},{2,50}... | collective-permute-start | bytes 786440 | tf_op jit(solution)/shard_map/ppermute | solution.py:110
  164.1 14.6 %collective-permute-start.5 = (bf16[256,1024]{1,0:T(8,128)(2,1)S(1)}, bf16[256,1024]{1,0:T(8,128)(2,1)S(1)}, u32[]{:S(2)}, u32[]{:S(2)}) collective-permute-start(bf16[256,1024]{1,0:T(8,128)(2,1)S(1)} %pad_maximum_fusion.2), channel_id=1, source_target_pairs={{0,16},{16,32},{32,48},{48,0},{1,17},{17,33},{33,49},{49,1},{2,18}... | collective-permute-start | bytes 1572872 | tf_op jit(solution)/shard_map/ppermute | solution.py:117
  166.3 14.2 %collective-permute-start.7 = (bf16[256,1024]{1,0:T(8,128)(2,1)S(1)}, bf16[256,1024]{1,0:T(8,128)(2,1)S(1)}, u32[]{:S(2)}, u32[]{:S(2)}) collective-permute-start(bf16[256,1024]{1,0:T(8,128)(2,1)S(1)} %pad_maximum_fusion.3), channel_id=1, source_target_pairs={{0,48},{16,0},{32,16},{48,32},{1,49},{17,1},{33,17},{49,33},{2,50}... | collective-permute-start | bytes 1572872 | tf_op jit(solution)/shard_map/ppermute | solution.py:118
  219.0 41.0 %all-to-all-start.4 = ((bf16[16,2,512]{2,1,0:T(2,128)(2,1)}), bf16[16,2,512]{2,1,0:T(2,128)(2,1)S(1)}, u32[]{:S(2)}, u32[]{:S(2)}) async-start(bf16[16,2,512]{2,1,0:T(2,128)(2,1)} %reshape.99), calls=%async_computation.5 | async-start | bytes 65536 | tf_op jit(solution)/shard_map/all_to_all | solution.py:124
  259.9 30.0 %all-to-all-start.2 = ((bf16[64,2,1536]{2,1,0:T(2,128)(2,1)}), bf16[64,2,1536]{2,1,0:T(2,128)(2,1)S(1)}, u32[]{:S(2)}, u32[]{:S(2)}) async-start(bf16[64,2,1536]{2,1,0:T(2,128)(2,1)} %reshape.101), calls=%async_computation.3 | async-start | bytes 786432 | tf_op jit(solution)/shard_map/all_to_all | solution.py:125
Sparse Core Ops, SparseCore 0:
  47.8 93.8 all-gather.3
  152.4 104.5 reduce-scatter.1

commit v3 on v2

--- a/solution.py
+++ b/solution.py
@@ -6,7 +6,7 @@
 EXP_GROUP = 8
 LANES = 128
 X_CHIPS = 4
-FRONT = 3072
+FRONT = 2304
 
 
 def on_device(tokens, expert_ids, gates, gate_weight, up_weight, down_weight):
@@ -52,9 +52,23 @@
         tiled=True,
     )
     front_all = lax.all_gather(front, "z", axis=0, tiled=True)
-    back_row, _ = lax.optimization_barrier((send_rows[:, FRONT:], front))
-    back = lax.all_to_all(back_row, "group", split_axis=0, concat_axis=0, tiled=True)
-    back_own = lax.all_gather(back, "z", axis=0, tiled=True)
+    back_row = jnp.concatenate(
+        [tokens[:, FRONT:], jnp.pad(chosen, ((0, 0), (0, LANES - groups)))], axis=1
+    )
+    back_row, _ = lax.optimization_barrier((back_row, front))
+    column = lax.all_gather(back_row, "z", axis=0, tiled=True)
+    tok_rows = tokens.shape[0]
+    same_z = (
+        jnp.arange(nz, dtype=jnp.int32)[:, None]
+        == jnp.arange(nz * tok_rows, dtype=jnp.int32)[None, :] // tok_rows
+    ).astype(jnp.bfloat16)
+    place = (column[:, width : width + groups].T[:, None, :] * same_z[None]).reshape(
+        groups * nz, nz * tok_rows
+    )
+    back = jnp.dot(place, column[:, :width], preferred_element_type=jnp.float32).astype(
+        jnp.bfloat16
+    )
+    back_own = lax.all_to_all(back, "group", split_axis=0, concat_axis=0, tiled=True)
     back_left = lax.ppermute(back_own, "x", to_right)
     back_right = lax.ppermute(back_own, "x", to_left)
     far_low = lax.ppermute(back_left[:, :half], "x", to_right)
@@ -74,14 +88,14 @@
             dot(far_low, both_back[:half]) + dot(far_high, both_back[half:]),
             dot(back_left, both_back),
         ]
-    ).reshape(nx, nz, groups, 2 * units)
+    ).reshape(nx, groups, nz, 2 * units)
     act_back = jnp.stack(
         [
             lax.dynamic_index_in_dim(by_offset, (x - x_me + nx) % nx, 0, keepdims=False)
             for x in range(nx)
         ],
         axis=2,
-    ).reshape(nz * groups * nx, 2 * units)
+    ).transpose(1, 0, 2, 3).reshape(nz * groups * nx, 2 * units)
     act = dot(front_all[:, :FRONT], both_front) + act_back
     hidden = (jax.nn.silu(act[:, :units]) * act[:, units:]).astype(jnp.bfloat16)
     mine = (x_me * nz + lax.axis_index("z")) // slices
@@ -98,8 +112,8 @@
     def block(offset):
         at = (x_me + offset) % nx
         return (
-            lax.dynamic_index_in_dim(hidden_x, at, 2, keepdims=False).reshape(rows_z, units),
-            lax.dynamic_index_in_dim(scale_x, at, 2, keepdims=False).reshape(rows_z, 1),
+            lax.dynamic_index_in_dim(hidden_x, at, 2, keepdims=False).swapaxes(0, 1).reshape(rows_z, units),
+            lax.dynamic_index_in_dim(scale_x, at, 2, keepdims=False).swapaxes(0, 1).reshape(rows_z, 1),
         )
 
     h_far, s_far = block(2)
@@ -117,16 +131,17 @@
     from_left = lax.ppermute(send_right, "x", to_right)
     from_right = lax.ppermute(send_left, "x", to_left)
     back_out = (dot(h_own, down[:, FRONT:]) * s_own + from_left + from_right).astype(jnp.bfloat16)
-    back_parts = lax.all_to_all(back_out, "z", split_axis=0, concat_axis=0, tiled=True)
-    back_sum = jnp.sum(
-        back_parts.reshape(nz, groups, width), axis=0, dtype=jnp.float32
+    back_group = lax.all_to_all(back_out, "group", split_axis=0, concat_axis=0, tiled=True)
+    back_tokens = jnp.einsum(
+        "rt,rd->td", place, back_group, preferred_element_type=jnp.float32
     ).astype(jnp.bfloat16)
-    back_home = lax.all_to_all(back_sum, "group", split_axis=0, concat_axis=0, tiled=True)
+    back_parts = lax.all_to_all(back_tokens, "z", split_axis=0, concat_axis=0, tiled=True)
+    back_home = jnp.sum(back_parts.reshape(nz, tok_rows, width), axis=0, dtype=jnp.float32)
     front_home = lax.all_to_all(
         front_z, ("group", "x"), split_axis=0, concat_axis=0, tiled=True
     )
     result = jnp.concatenate(
-        [dot(jnp.repeat(chosen, nx, axis=1), front_home), dot(chosen, back_home)], axis=1
+        [dot(jnp.repeat(chosen, nx, axis=1), front_home), back_home], axis=1
     )
     return result.astype(jnp.bfloat16)
 

time: 299 us -> 295 us (0.987)
  starting transfers between devices: 52.8 us -> 35.8 us
  blocking collectives: 121 us -> 131 us
    reduce_scatter x1, waiting for transfers between devices: 24.6 us -> 0.02 us  [on_device(): front_z = lax.psum_scatter(front_out, 'z', scatter_dimension=0, tiled=True)]
    all_to_all x2, blocking collectives: 48.7 us -> 68.5 us  [the longest x1 36.6 us: on_device(): lax.all_to_all(back, 'group', split_axis=0, concat_axis=0, tiled=True)]
    all_gather x1, waiting for transfers between devices: 14.5 us -> 0.01 us  [on_device(): front_all = lax.all_gather(front, 'z', axis=0, tiled=True)]
    all_to_all x1, waiting for transfers between devices: 0.01 us -> 13.6 us  [on_device(): lax.all_to_all(back_tokens, 'z', split_axis=0, concat_axis=0, tiled=True)]
    ppermute x1, waiting for transfers between devices: 5.61 us -> 18 us  [on_device(): back_right = lax.ppermute(back_own, 'x', to_left)]
    all_to_all x1, starting transfers between devices: 13.4 us -> 3.76 us  [on_device(): lax.all_to_all(back_tokens, 'z', split_axis=0, concat_axis=0, tiled=True)]
    ppermute x1, waiting for transfers between devices: 7.38 us -> 15.3 us  [on_device(): from_left = lax.ppermute(send_right, 'x', to_right)]
    all_to_all x1, starting transfers between devices: 15.3 us -> 7.81 us  [on_device(): lax.all_to_all(front_z, ('group', 'x'), split_axis=0, concat_axis=0, tile...]
  transfers between devices with their start and end apart: 12 -> 12, of which waited for: 8 -> 8; matrix products, arithmetic and copies ran while one was open for 5% -> 6% of each run, Pallas kernels for 0% -> 0%
where the time goes in v3:
time: 295 us; the launch traced here: 293 us
  blocking collectives  131 us (44%)
  waiting for transfers between devices  75.6 us (26%)
  starting transfers between devices  35.8 us (12%)
  matrix products  15.6 us (5%)
  between operations  14 us (5%)
  local copies, waits for them, and re-layouts  10.6 us (4%)
  other arithmetic  10.3 us (3%)
    all_to_all x1, blocking collectives, on_device(): lax.all_to_all(back, 'group', split_axis=0, concat_axis=0, tiled=True)  36.6 us
    all_gather x1, blocking collectives, on_device(): column = lax.all_gather(back_row, 'z', axis=0, tiled=True)  32 us
    all_to_all x1, blocking collectives, on_device(): lax.all_to_all(back_out, 'group', split_axis=0, concat_axis=0, tiled=True)  31.9 us
    all_to_all x1, blocking collectives, on_device(): lax.all_to_all(jnp.broadcast_to(front_row[:, None], (groups, nx, FRONT +...  30.9 us
    ppermute x1, waiting for transfers between devices, on_device(): back_right = lax.ppermute(back_own, 'x', to_left)  18 us
    ppermute x1, waiting for transfers between devices, on_device(): from_left = lax.ppermute(send_right, 'x', to_right)  15.3 us
    dot_general x15, matrix products, dot(): return jnp.dot(a, b, preferred_element_type=jnp.float32)  13.9 us
    all_to_all x1, waiting for transfers between devices, on_device(): lax.all_to_all(back_tokens, 'z', split_axis=0, concat_axis=0, tiled=True)  13.6 us
  transfers between devices with their start and end apart: 12, of which 8 were waited for; matrix products, arithmetic and copies ran while one was open for 6% of the time, Pallas kernels for 0%

profile of v3, /device:TPU:1, one launch (start us, length us, event | category | flops | bytes accessed | tf_op | source)
XLA Modules:
  0.0 293.3 jit_solution(17780982678722956961)
XLA Ops:
  10.2 2.5 reduce.9
  13.0 30.9 %all_to_all.55 = bf16[64,2,1216]{2,1,0:T(2,128)(2,1)S(1)} all-to-all(bf16[64,2,1216]{2,1,0:T(2,128)(2,1)S(1)} %reshape.158), channel_id=1, replica_groups=mesh['group'=16,'x'=4,'z'=16] {'group','x'}, dimensions={0} | all-to-all | bytes 622592 | tf_op jit(solution)/shard_map/all_to_all | solution.py:45
  45.2 32.0 %all-gather.1 = bf16[16,4,1920]{2,1,0:T(4,128)(2,1)S(1)} all-gather(bf16[1,4,1920]{2,1,0:T(4,128)(2,1)S(1)} %bitcast.135), channel_id=1, replica_groups=mesh['group'=16,'x'=4,'z'=16] {'z'}, dimensions={0}, use_global_device_ids=true | all-gather | bytes 261120 | tf_op jit(solution)/shard_map/all_gather | solution.py:59
  77.8 36.6 %all_to_all.56 = bf16[16,16,1792]{2,1,0:T(8,128)(2,1)S(1)} all-to-all(bf16[16,16,1792]{2,1,0:T(8,128)(2,1)S(1)} %bitcast.119), channel_id=1, replica_groups=mesh['group'=16,'x'=4,'z'=16] {'group'}, dimensions={0} | all-to-all | bytes 1835008 | tf_op jit(solution)/shard_map/all_to_all | solution.py:71
  114.4 2.9 collective-permute-start
  117.3 2.4 collective-permute-start.1
  120.3 18.0 %collective-permute-done = bf16[256,1792]{1,0:T(8,128)(2,1)} collective-permute-done((bf16[256,1792]{1,0:T(8,128)(2,1)S(1)}, bf16[256,1792]{1,0:T(8,128)(2,1)}, u32[]{:S(2)}, u32[]{:S(2)}) %collective-permute-start) | collective-permute-done | bytes 917536 | tf_op jit(solution)/shard_map/ppermute | solution.py:73
  139.4 3.8 %collective-permute-start.3 = (bf16[256,896]{1,0:T(8,128)(2,1)S(1)}, bf16[256,896]{1,0:T(8,128)(2,1)S(1)}, u32[]{:S(2)}, u32[]{:S(2)}) collective-permute-start(bf16[256,896]{1,0:T(8,128)(2,1)S(1)} %slice.85), channel_id=1, source_target_pairs={{0,48},{16,0},{32,16},{48,32},{1,49},{17,1},{33,17},{49,33},{2,50}... | collective-permute-start | bytes 1376264 | tf_op jit(solution)/shard_map/ppermute | solution.py:75
  144.3 2.1 collective-permute-start.2
  149.6 3.8 %collective-permute-done.3 = bf16[256,896]{1,0:T(8,128)(2,1)S(1)} collective-permute-done((bf16[256,896]{1,0:T(8,128)(2,1)S(1)}, bf16[256,896]{1,0:T(8,128)(2,1)S(1)}, u32[]{:S(2)}, u32[]{:S(2)}) %collective-permute-start.3) | collective-permute-done | bytes 458784 | tf_op jit(solution)/shard_map/ppermute | solution.py:75
  153.7 5.1 %collective-permute-done.2 = bf16[256,896]{1,0:T(8,128)(2,1)S(1)} collective-permute-done((bf16[256,896]{1,0:T(8,128)(2,1)S(1)}, bf16[256,896]{1,0:T(8,128)(2,1)S(1)}, u32[]{:S(2)}, u32[]{:S(2)}) %collective-permute-start.2) | collective-permute-done | bytes 458784 | tf_op jit(solution)/shard_map/ppermute | solution.py:74
  161.5 4.0 %fusion.3 = f32[1024,256]{1,0:T(8,128)S(1)} fusion(f32[1024,256]{1,0:T(8,128)} %reshape.143, bf16[1024,2432]{1,0:T(8,128)(2,1)} %bitcast.140, bf16[4096,128]{1,0:T(8,128)(2,1)S(1)} %bitcast.105, bf16[4096,128]{1,0:T(8,128)(2,1)S(1)} %bitcast.109), kind=kOutput, calls=%fused_computation.15 | convolution fusion | flops 1210580992 | bytes 8912896 | tf_op jit(solution)/shard_map/dot_general | solution.py:81
  166.9 3.5 %multiply_convert_fusion = bf16[1024,2304]{1,0:T(8,128)(2,1)} fusion(bf16[1024,128]{1,0:T(8,128)(2,1)S(1)} %get-tuple-element.23, f32[1024]{0:T(1024)S(1)} %get-tuple-element.24, bf16[128,4096]{1,0:T(8,128)(2,1)S(1)} %bitcast.111), kind=kOutput, calls=%fused_computation | convolution fusion | flops 608698368 | bytes 5574656 | tf_op jit(solution)/shard_map/dot_general | solution.py:81
  172.0 1.9 collective-permute-start.4
  174.6 4.6 %collective-permute-start.6 = (bf16[256,896]{1,0:T(8,128)(2,1)S(1)}, bf16[256,896]{1,0:T(8,128)(2,1)S(1)}, u32[]{:S(2)}, u32[]{:S(2)}) collective-permute-start(bf16[256,896]{1,0:T(8,128)(2,1)S(1)} %fusion.9), channel_id=1, source_target_pairs={{0,48},{16,0},{32,16},{48,32},{1,49},{17,1},{33,17},{49,33},{2,50}... | collective-permute-start | bytes 1376264 | tf_op jit(solution)/shard_map/ppermute | solution.py:124
  179.8 6.0 %collective-permute-done.4 = bf16[256,896]{1,0:T(8,128)(2,1)S(1)} collective-permute-done((bf16[256,896]{1,0:T(8,128)(2,1)S(1)}, bf16[256,896]{1,0:T(8,128)(2,1)S(1)}, u32[]{:S(2)}, u32[]{:S(2)}) %collective-permute-start.4) | collective-permute-done | bytes 458784 | tf_op jit(solution)/shard_map/ppermute | solution.py:123
  186.1 1.9 collective-permute-start.5
  188.4 4.6 %collective-permute-start.7 = (bf16[256,1792]{1,0:T(8,128)(2,1)S(1)}, bf16[256,1792]{1,0:T(8,128)(2,1)}, u32[]{:S(2)}, u32[]{:S(2)}) collective-permute-start(bf16[256,1792]{1,0:T(8,128)(2,1)S(1)} %pad_maximum_fusion.2), channel_id=1, source_target_pairs={{0,48},{16,0},{32,16},{48,32},{1,49},{17,1},{33,17},{49,33},{2,50}... | collective-permute-start | bytes 2752520 | tf_op jit(solution)/shard_map/ppermute | solution.py:132
  193.6 15.3 %collective-permute-done.5 = bf16[256,1792]{1,0:T(8,128)(2,1)} collective-permute-done((bf16[256,1792]{1,0:T(8,128)(2,1)S(1)}, bf16[256,1792]{1,0:T(8,128)(2,1)}, u32[]{:S(2)}, u32[]{:S(2)}) %collective-permute-start.5) | collective-permute-done | bytes 917536 | tf_op jit(solution)/shard_map/ppermute | solution.py:131
  211.8 31.9 %all_to_all.57 = bf16[16,16,1792]{2,1,0:T(8,128)(2,1)S(1)} all-to-all(bf16[16,16,1792]{2,1,0:T(8,128)(2,1)S(1)} %bitcast.122), channel_id=1, replica_groups=mesh['group'=16,'x'=4,'z'=16] {'group'}, dimensions={0} | all-to-all | bytes 1835008 | tf_op jit(solution)/shard_map/all_to_all | solution.py:134
  244.7 3.8 %all-to-all-start.4 = ((bf16[16,4,1792]{2,1,0:T(4,128)(2,1)}), bf16[16,4,1792]{2,1,0:T(4,128)(2,1)S(1)}, u32[]{:S(2)}, u32[]{:S(2)}) async-start(bf16[16,4,1792]{2,1,0:T(4,128)(2,1)} %all_to_all.47), calls=%async_computation.5 | async-start | bytes 458752 | tf_op jit(solution)/shard_map/all_to_all | solution.py:138
  251.1 13.6 %all-to-all-done.4 = bf16[16,4,1792]{2,1,0:T(4,128)(2,1)S(1)} async-done(((bf16[16,4,1792]{2,1,0:T(4,128)(2,1)}), bf16[16,4,1792]{2,1,0:T(4,128)(2,1)S(1)}, u32[]{:S(2)}, u32[]{:S(2)}) %all-to-all-start.4) | async-done | bytes 229408 | tf_op jit(solution)/shard_map/all_to_all | solution.py:138
  264.7 7.8 %all-to-all-start.2 = ((bf16[64,2,1152]{2,1,0:T(2,128)(2,1)}), bf16[64,2,1152]{2,1,0:T(2,128)(2,1)S(1)}, u32[]{:S(2)}, u32[]{:S(2)}) async-start(bf16[64,2,1152]{2,1,0:T(2,128)(2,1)} %reshape.160), calls=%async_computation.3 | async-start | bytes 589824 | tf_op jit(solution)/shard_map/all_to_all | solution.py:140
  272.8 12.6 %all-to-all-done.2 = bf16[64,2,1152]{2,1,0:T(2,128)(2,1)S(1)} async-done(((bf16[64,2,1152]{2,1,0:T(2,128)(2,1)}), bf16[64,2,1152]{2,1,0:T(2,128)(2,1)S(1)}, u32[]{:S(2)}, u32[]{:S(2)}) %all-to-all-start.2) | async-done | bytes 294944 | tf_op jit(solution)/shard_map/all_to_all | solution.py:140
  (92 shorter events, 27.7 us)
Async XLA Ops:
  6.5 154.9 %all-gather.4.cloned.1.call-start = ((), (), s32[]{:S(2)}) async-start(), calls=%async_computation.7 | async-start | bytes 5292032 | tf_op jit(solution)/shard_map/all_gather | solution.py:54
  12.7 32.5 %slice-start = ((bf16[4,4096]{1,0:T(4,128)(2,1)}), bf16[4,1792]{1,0:T(4,128)(2,1)S(1)}, s32[]{:S(2)}) async-start(bf16[4,4096]{1,0:T(4,128)(2,1)} %param.6), calls=%async_computation.8 | async-start | bytes 28672 | tf_op jit(solution)/shard_map/slice | solution.py:56
  45.2 203.4 %reduce-scatter.2.cloned.1.call-start = ((), (), s32[]{:S(2)}) async-start(), calls=%async_computation.6 | async-start | bytes 5013504 | tf_op jit(solution)/shard_map/reduce_scatter | solution.py:107
  77.2 42.6 %copy-start = (bf16[1,4096,128]{2,1,0:T(8,128)(2,1)S(1)}, bf16[1,4096,128]{2,1,0:T(8,128)(2,1)}, u32[]{:S(2)}) copy-start(bf16[1,4096,128]{2,1,0:T(8,128)(2,1)} %param.9) | copy-start | bytes 3145732
  77.2 42.6 %copy-start.1 = (bf16[1,4096,128]{2,1,0:T(8,128)(2,1)S(1)}, bf16[1,4096,128]{2,1,0:T(8,128)(2,1)}, u32[]{:S(2)}) copy-start(bf16[1,4096,128]{2,1,0:T(8,128)(2,1)} %param.10) | copy-start | bytes 3145732
  114.4 23.9 %collective-permute-start = (bf16[256,1792]{1,0:T(8,128)(2,1)S(1)}, bf16[256,1792]{1,0:T(8,128)(2,1)}, u32[]{:S(2)}, u32[]{:S(2)}) collective-permute-start(bf16[256,1792]{1,0:T(8,128)(2,1)S(1)} %bitcast.120), channel_id=1, source_target_pairs={{0,48},{16,0},{32,16},{48,32},{1,49},{17,1},{33,17},{49,33},{2,50}... | collective-permute-start | bytes 2752520 | tf_op jit(solution)/shard_map/ppermute | solution.py:73
  117.3 25.9 %collective-permute-start.1 = (bf16[256,1792]{1,0:T(8,128)(2,1)S(1)}, bf16[256,1792]{1,0:T(8,128)(2,1)}, u32[]{:S(2)}, u32[]{:S(2)}) collective-permute-start(bf16[256,1792]{1,0:T(8,128)(2,1)S(1)} %bitcast.121), channel_id=1, source_target_pairs={{0,16},{16,32},{32,48},{48,0},{1,17},{17,33},{33,49},{49,1},{2,18}... | collective-permute-start | bytes 2752520 | tf_op jit(solution)/shard_map/ppermute | solution.py:72
  139.4 14.0 %collective-permute-start.3 = (bf16[256,896]{1,0:T(8,128)(2,1)S(1)}, bf16[256,896]{1,0:T(8,128)(2,1)S(1)}, u32[]{:S(2)}, u32[]{:S(2)}) collective-permute-start(bf16[256,896]{1,0:T(8,128)(2,1)S(1)} %slice.85), channel_id=1, source_target_pairs={{0,48},{16,0},{32,16},{48,32},{1,49},{17,1},{33,17},{49,33},{2,50}... | collective-permute-start | bytes 1376264 | tf_op jit(solution)/shard_map/ppermute | solution.py:75
  144.3 14.5 %collective-permute-start.2 = (bf16[256,896]{1,0:T(8,128)(2,1)S(1)}, bf16[256,896]{1,0:T(8,128)(2,1)S(1)}, u32[]{:S(2)}, u32[]{:S(2)}) collective-permute-start(bf16[256,896]{1,0:T(8,128)(2,1)S(1)} %slice.82), channel_id=1, source_target_pairs={{0,16},{16,32},{32,48},{48,0},{1,17},{17,33},{33,49},{49,1},{2,18}... | collective-permute-start | bytes 1376264 | tf_op jit(solution)/shard_map/ppermute | solution.py:74
  165.5 1.3 copy-start.2
  172.0 13.7 %collective-permute-start.4 = (bf16[256,896]{1,0:T(8,128)(2,1)S(1)}, bf16[256,896]{1,0:T(8,128)(2,1)S(1)}, u32[]{:S(2)}, u32[]{:S(2)}) collective-permute-start(bf16[256,896]{1,0:T(8,128)(2,1)S(1)} %fusion.6), channel_id=1, source_target_pairs={{0,16},{16,32},{32,48},{48,0},{1,17},{17,33},{33,49},{49,1},{2,18}... | collective-permute-start | bytes 1376264 | tf_op jit(solution)/shard_map/ppermute | solution.py:123
  174.6 13.4 %collective-permute-start.6 = (bf16[256,896]{1,0:T(8,128)(2,1)S(1)}, bf16[256,896]{1,0:T(8,128)(2,1)S(1)}, u32[]{:S(2)}, u32[]{:S(2)}) collective-permute-start(bf16[256,896]{1,0:T(8,128)(2,1)S(1)} %fusion.9), channel_id=1, source_target_pairs={{0,48},{16,0},{32,16},{48,32},{1,49},{17,1},{33,17},{49,33},{2,50}... | collective-permute-start | bytes 1376264 | tf_op jit(solution)/shard_map/ppermute | solution.py:124
  186.1 22.7 %collective-permute-start.5 = (bf16[256,1792]{1,0:T(8,128)(2,1)S(1)}, bf16[256,1792]{1,0:T(8,128)(2,1)}, u32[]{:S(2)}, u32[]{:S(2)}) collective-permute-start(bf16[256,1792]{1,0:T(8,128)(2,1)S(1)} %pad_maximum_fusion.1), channel_id=1, source_target_pairs={{0,16},{16,32},{32,48},{48,0},{1,17},{17,33},{33,49},{49,1},{2,18}... | collective-permute-start | bytes 2752520 | tf_op jit(solution)/shard_map/ppermute | solution.py:131
  188.4 21.6 %collective-permute-start.7 = (bf16[256,1792]{1,0:T(8,128)(2,1)S(1)}, bf16[256,1792]{1,0:T(8,128)(2,1)}, u32[]{:S(2)}, u32[]{:S(2)}) collective-permute-start(bf16[256,1792]{1,0:T(8,128)(2,1)S(1)} %pad_maximum_fusion.2), channel_id=1, source_target_pairs={{0,48},{16,0},{32,16},{48,32},{1,49},{17,1},{33,17},{49,33},{2,50}... | collective-permute-start | bytes 2752520 | tf_op jit(solution)/shard_map/ppermute | solution.py:132
  244.7 20.0 %all-to-all-start.4 = ((bf16[16,4,1792]{2,1,0:T(4,128)(2,1)}), bf16[16,4,1792]{2,1,0:T(4,128)(2,1)S(1)}, u32[]{:S(2)}, u32[]{:S(2)}) async-start(bf16[16,4,1792]{2,1,0:T(4,128)(2,1)} %all_to_all.47), calls=%async_computation.5 | async-start | bytes 458752 | tf_op jit(solution)/shard_map/all_to_all | solution.py:138
  264.7 20.7 %all-to-all-start.2 = ((bf16[64,2,1152]{2,1,0:T(2,128)(2,1)}), bf16[64,2,1152]{2,1,0:T(2,128)(2,1)S(1)}, u32[]{:S(2)}, u32[]{:S(2)}) async-start(bf16[64,2,1152]{2,1,0:T(2,128)(2,1)} %reshape.160), calls=%async_computation.3 | async-start | bytes 589824 | tf_op jit(solution)/shard_map/all_to_all | solution.py:140
Sparse Core Ops, SparseCore 0:
  45.3 74.8 all-gather.3
  170.5 63.1 reduce-scatter.1

commit v4 on v3

--- a/solution.py
+++ b/solution.py
@@ -6,7 +6,8 @@
 EXP_GROUP = 8
 LANES = 128
 X_CHIPS = 4
-FRONT = 2304
+FRONT = 2048
+FRONT_OUT = 2560
 
 
 def on_device(tokens, expert_ids, gates, gate_weight, up_weight, down_weight):
@@ -42,21 +43,23 @@
         [send_rows[:, :FRONT], jnp.pad(gate_table, ((0, 0), (0, LANES - EXP_GROUP)))], axis=1
     )
 
+    back_row = jnp.concatenate(
+        [tokens[:, FRONT:], jnp.pad(chosen, ((0, 0), (0, LANES - groups)))], axis=1
+    )
+    front_send = jnp.broadcast_to(front_row[:, None], (groups, nx, FRONT + LANES)).reshape(
+        groups * nx, FRONT + LANES
+    )
+    back_row, front_send = lax.optimization_barrier((back_row, front_send))
+    column = lax.all_gather(back_row, "z", axis=0, tiled=True)
     front = lax.all_to_all(
-        jnp.broadcast_to(front_row[:, None], (groups, nx, FRONT + LANES)).reshape(
-            groups * nx, FRONT + LANES
-        ),
+        front_send,
         ("group", "x"),
         split_axis=0,
         concat_axis=0,
         tiled=True,
     )
+    front, column = lax.optimization_barrier((front, column))
     front_all = lax.all_gather(front, "z", axis=0, tiled=True)
-    back_row = jnp.concatenate(
-        [tokens[:, FRONT:], jnp.pad(chosen, ((0, 0), (0, LANES - groups)))], axis=1
-    )
-    back_row, _ = lax.optimization_barrier((back_row, front))
-    column = lax.all_gather(back_row, "z", axis=0, tiled=True)
     tok_rows = tokens.shape[0]
     same_z = (
         jnp.arange(nz, dtype=jnp.int32)[:, None]
@@ -69,13 +72,17 @@
         jnp.bfloat16
     )
     back_own = lax.all_to_all(back, "group", split_axis=0, concat_axis=0, tiled=True)
-    back_left = lax.ppermute(back_own, "x", to_right)
-    back_right = lax.ppermute(back_own, "x", to_left)
-    far_low = lax.ppermute(back_left[:, :half], "x", to_right)
-    far_high = lax.ppermute(back_right[:, half:], "x", to_left)
+    own_low, own_high = back_own[:, :half], back_own[:, half:]
+    left_low = lax.ppermute(own_low, "x", to_right)
+    right_high = lax.ppermute(own_high, "x", to_left)
+    left_high = lax.ppermute(own_high, "x", to_right)
+    right_low = lax.ppermute(own_low, "x", to_left)
+    far_low = lax.ppermute(left_low, "x", to_right)
+    far_high = lax.ppermute(right_high, "x", to_left)
 
     both = jnp.concatenate([gate_weight[0], up_weight[0]], axis=1)
     both_front, both_back = both[:FRONT], both[FRONT:]
+    back_low, back_high = both_back[:half], both_back[half:]
 
     def dot(a, b):
         return jnp.dot(a, b, preferred_element_type=jnp.float32)
@@ -84,9 +91,9 @@
     by_offset = jnp.stack(
         [
             dot(back_own, both_back),
-            dot(back_right, both_back),
-            dot(far_low, both_back[:half]) + dot(far_high, both_back[half:]),
-            dot(back_left, both_back),
+            dot(right_low, back_low) + dot(right_high, back_high),
+            dot(far_low, back_low) + dot(far_high, back_high),
+            dot(left_low, back_low) + dot(left_high, back_high),
         ]
     ).reshape(nx, groups, nz, 2 * units)
     act_back = jnp.stack(
@@ -103,9 +110,11 @@
     scale = jnp.sum(front_all[:, FRONT:].astype(jnp.float32) * own[None, :], axis=1, keepdims=True)
 
     down = down_weight[0]
-    front_out = (dot(hidden, down[:, :FRONT]) * scale).astype(jnp.bfloat16)
+    front_out = (dot(hidden, down[:, :FRONT_OUT]) * scale).astype(jnp.bfloat16)
     front_z = lax.psum_scatter(front_out, "z", scatter_dimension=0, tiled=True)
-    down_low, down_high = down[:, FRONT : FRONT + half], down[:, FRONT + half :]
+    out_width = features - FRONT_OUT
+    middle = FRONT_OUT + out_width // 2
+    down_low, down_high = down[:, FRONT_OUT:middle], down[:, middle:]
     hidden_x = hidden.reshape(nz, groups, nx, units)
     scale_x = scale.reshape(nz, groups, nx, 1)
 
@@ -120,23 +129,29 @@
     h_right, s_right = block(1)
     h_left, s_left = block(3)
     h_own, s_own = block(0)
-    low_in = lax.ppermute((dot(h_far, down_low) * s_far).astype(jnp.bfloat16), "x", to_right)
-    high_in = lax.ppermute((dot(h_far, down_high) * s_far).astype(jnp.bfloat16), "x", to_left)
-    send_right = jnp.concatenate(
-        [dot(h_right, down_low) * s_right + low_in, dot(h_right, down_high) * s_right], axis=1
-    ).astype(jnp.bfloat16)
-    send_left = jnp.concatenate(
-        [dot(h_left, down_low) * s_left, dot(h_left, down_high) * s_left + high_in], axis=1
-    ).astype(jnp.bfloat16)
-    from_left = lax.ppermute(send_right, "x", to_right)
-    from_right = lax.ppermute(send_left, "x", to_left)
-    back_out = (dot(h_own, down[:, FRONT:]) * s_own + from_left + from_right).astype(jnp.bfloat16)
+
+    def part(h, s, weights, more=0.0):
+        return (dot(h, weights) * s + more).astype(jnp.bfloat16)
+
+    low_in = lax.ppermute(part(h_far, s_far, down_low), "x", to_right)
+    high_in = lax.ppermute(part(h_far, s_far, down_high), "x", to_left)
+    left_high_in = lax.ppermute(part(h_right, s_right, down_high), "x", to_right)
+    right_low_in = lax.ppermute(part(h_left, s_left, down_low), "x", to_left)
+    left_low_in = lax.ppermute(part(h_right, s_right, down_low, low_in), "x", to_right)
+    right_high_in = lax.ppermute(part(h_left, s_left, down_high, high_in), "x", to_left)
+    back_out = jnp.concatenate(
+        [
+            part(h_own, s_own, down_low, left_low_in.astype(jnp.float32) + right_low_in),
+            part(h_own, s_own, down_high, left_high_in.astype(jnp.float32) + right_high_in),
+        ],
+        axis=1,
+    )
     back_group = lax.all_to_all(back_out, "group", split_axis=0, concat_axis=0, tiled=True)
     back_tokens = jnp.einsum(
         "rt,rd->td", place, back_group, preferred_element_type=jnp.float32
     ).astype(jnp.bfloat16)
     back_parts = lax.all_to_all(back_tokens, "z", split_axis=0, concat_axis=0, tiled=True)
-    back_home = jnp.sum(back_parts.reshape(nz, tok_rows, width), axis=0, dtype=jnp.float32)
+    back_home = jnp.sum(back_parts.reshape(nz, tok_rows, out_width), axis=0, dtype=jnp.float32)
     front_home = lax.all_to_all(
         front_z, ("group", "x"), split_axis=0, concat_axis=0, tiled=True
     )

time: 295 us -> 283 us (0.959)
  blocking collectives: 131 us -> 101 us
  starting transfers between devices: 35.8 us -> 65.6 us
  waiting for transfers between devices: 75.6 us -> 65.7 us
  other arithmetic: 10.3 us -> 6.83 us
    all_to_all x1 -> x0, blocking collectives: 30.9 us -> none  [on_device(): lax.all_to_all(jnp.broadcast_to(front_row[:, None], (groups, nx, FRONT +...]
    all_to_all x0 -> x1, starting transfers between devices: none -> 18.2 us  [on_device(): lax.all_to_all(front_send, ('group', 'x'), split_axis=0, concat_axis=0, t...]
    ppermute x8 -> x12, starting transfers between devices: 24.2 us -> 36.9 us  [the longest x1 5.31 us: on_device(): far_high = lax.ppermute(right_high, 'x', to_left)]
    ppermute x8 -> x12, waiting for transfers between devices: 49.3 us -> 40.7 us  [the longest x1 10.2 us: on_device(): far_low = lax.ppermute(left_low, 'x', to_right)]
    all_to_all x1, blocking collectives: 36.6 us -> 42.7 us  [on_device(): lax.all_to_all(back, 'group', split_axis=0, concat_axis=0, tiled=True)]
    all_to_all x1, blocking collectives: 31.9 us -> 28.2 us  [on_device(): lax.all_to_all(back_out, 'group', split_axis=0, concat_axis=0, tiled=True)]
    dot_general x15 -> x18, matrix products: 13.9 us -> 14.4 us  [dot(): return jnp.dot(a, b, preferred_element_type=jnp.float32)]
  transfers between devices with their start and end apart: 12 -> 17, of which waited for: 8 -> 9; matrix products, arithmetic and copies ran while one was open for 6% -> 6% of each run, Pallas kernels for 0% -> 0%
where the time goes in v4:
time: 283 us; the launch traced here: 281 us
  blocking collectives  101 us (36%)
  waiting for transfers between devices  65.7 us (23%)
  starting transfers between devices  65.6 us (23%)
  matrix products  16 us (6%)
  between operations  14.1 us (5%)
  local copies, waits for them, and re-layouts  11.8 us (4%)
  other arithmetic  6.83 us (2%)
    all_to_all x1, blocking collectives, on_device(): lax.all_to_all(back, 'group', split_axis=0, concat_axis=0, tiled=True)  42.7 us
    all_gather x1, blocking collectives, on_device(): column = lax.all_gather(back_row, 'z', axis=0, tiled=True)  30.5 us
    all_to_all x1, blocking collectives, on_device(): lax.all_to_all(back_out, 'group', split_axis=0, concat_axis=0, tiled=True)  28.2 us
    all_to_all x1, starting transfers between devices, on_device(): lax.all_to_all(front_send, ('group', 'x'), split_axis=0, concat_axis=0, t...  18.2 us
    dot_general x18, matrix products, dot(): return jnp.dot(a, b, preferred_element_type=jnp.float32)  14.4 us
    all_to_all x1, waiting for transfers between devices, on_device(): lax.all_to_all(front_z, ('group', 'x'), split_axis=0, concat_axis=0, tile...  13.1 us
    all_to_all x1, waiting for transfers between devices, on_device(): lax.all_to_all(back_tokens, 'z', split_axis=0, concat_axis=0, tiled=True)  11.8 us
    ppermute x1, waiting for transfers between devices, on_device(): far_low = lax.ppermute(left_low, 'x', to_right)  10.2 us
  transfers between devices with their start and end apart: 17, of which 9 were waited for; matrix products, arithmetic and copies ran while one was open for 6% of the time, Pallas kernels for 0%

profile of v4, /device:TPU:1, one launch (start us, length us, event | category | flops | bytes accessed | tf_op | source)
XLA Modules:
  0.0 281.5 jit_solution(7237968432692004240)
XLA Ops:
  12.5 18.2 %all-to-all-start = ((bf16[64,2,1088]{2,1,0:T(2,128)(2,1)}), bf16[64,2,1088]{2,1,0:T(2,128)(2,1)S(1)}, u32[]{:S(2)}, u32[]{:S(2)}) async-start(bf16[64,2,1088]{2,1,0:T(2,128)(2,1)} %reshape.159), calls=%async_computation | async-start | bytes 589824 | tf_op jit(solution)/shard_map/all_to_all | solution.py:54
  30.8 30.5 %all-gather = bf16[16,4,2176]{2,1,0:T(4,128)(2,1)S(1)} all-gather(bf16[1,4,2176]{2,1,0:T(4,128)(2,1)S(1)} %bitcast.149), channel_id=1, replica_groups=mesh['group'=16,'x'=4,'z'=16] {'z'}, dimensions={0}, use_global_device_ids=true | all-gather | bytes 295936 | tf_op jit(solution)/shard_map/all_gather | solution.py:53
  63.1 42.7 %all_to_all.54 = bf16[16,16,2048]{2,1,0:T(8,128)(2,1)S(1)} all-to-all(bf16[16,16,2048]{2,1,0:T(8,128)(2,1)S(1)} %bitcast.132), channel_id=1, replica_groups=mesh['group'=16,'x'=4,'z'=16] {'group'}, dimensions={0} | all-to-all | bytes 2097152 | tf_op jit(solution)/shard_map/all_to_all | solution.py:74
  107.9 4.3 %collective-permute-start.1 = (bf16[256,1024]{1,0:T(8,128)(2,1)}, bf16[256,1024]{1,0:T(8,128)(2,1)S(1)}, u32[]{:S(2)}, u32[]{:S(2)}) collective-permute-start(bf16[256,1024]{1,0:T(8,128)(2,1)} %get-tuple-element.24), channel_id=1, source_target_pairs={{0,48},{16,0},{32,16},{48,32},{1,49},{17,1},{33,17},{49,33},{2,50}... | collective-permute-start | bytes 1572872 | tf_op jit(solution)/shard_map/ppermute | solution.py:77
  112.3 1.9 collective-permute-start.5
  114.3 2.1 collective-permute-start.2
  116.5 4.3 %collective-permute-start = (bf16[256,1024]{1,0:T(8,128)(2,1)}, bf16[256,1024]{1,0:T(8,128)(2,1)S(1)}, u32[]{:S(2)}, u32[]{:S(2)}) collective-permute-start(bf16[256,1024]{1,0:T(8,128)(2,1)} %get-tuple-element.23), channel_id=1, source_target_pairs={{0,48},{16,0},{32,16},{48,32},{1,49},{17,1},{33,17},{49,33},{2,50}... | collective-permute-start | bytes 1572872 | tf_op jit(solution)/shard_map/ppermute | solution.py:79
  124.2 5.3 %collective-permute-start.4 = (bf16[256,1024]{1,0:T(8,128)(2,1)S(1)}, bf16[256,1024]{1,0:T(8,128)(2,1)S(1)}, u32[]{:S(2)}, u32[]{:S(2)}) collective-permute-start(bf16[256,1024]{1,0:T(8,128)(2,1)S(1)} %collective-permute-done.1), channel_id=1, source_target_pairs={{0,48},{16,0},{32,16},{48,32},{1,49},{17,1},{33,17},{49,33},{2,50}... | collective-permute-start | bytes 1572872 | tf_op jit(solution)/shard_map/ppermute | solution.py:81
  131.2 8.9 %collective-permute-done.2 = bf16[256,1024]{1,0:T(8,128)(2,1)S(1)} collective-permute-done((bf16[256,1024]{1,0:T(8,128)(2,1)}, bf16[256,1024]{1,0:T(8,128)(2,1)S(1)}, u32[]{:S(2)}, u32[]{:S(2)}) %collective-permute-start.2) | collective-permute-done | bytes 524320 | tf_op jit(solution)/shard_map/ppermute | solution.py:76
  142.6 3.3 %collective-permute-done.4 = bf16[256,1024]{1,0:T(8,128)(2,1)S(1)} collective-permute-done((bf16[256,1024]{1,0:T(8,128)(2,1)S(1)}, bf16[256,1024]{1,0:T(8,128)(2,1)S(1)}, u32[]{:S(2)}, u32[]{:S(2)}) %collective-permute-start.4) | collective-permute-done | bytes 524320 | tf_op jit(solution)/shard_map/ppermute | solution.py:81
  146.2 10.2 %collective-permute-done.3 = bf16[256,1024]{1,0:T(8,128)(2,1)S(1)} collective-permute-done((bf16[256,1024]{1,0:T(8,128)(2,1)S(1)}, bf16[256,1024]{1,0:T(8,128)(2,1)S(1)}, u32[]{:S(2)}, u32[]{:S(2)}) %collective-permute-start.3) | collective-permute-done | bytes 524320 | tf_op jit(solution)/shard_map/ppermute | solution.py:80
  159.0 3.8 %fusion.3 = f32[1024,256]{1,0:T(8,128)S(1)} fusion(f32[1024,256]{1,0:T(8,128)} %reshape.145, bf16[1024,2176]{1,0:T(8,128)(2,1)} %all-gather.3.cloned.1.call-done, bf16[4096,128]{1,0:T(8,128)(2,1)S(1)} %bitcast.120, bf16[4096,128]{1,0:T(8,128)(2,1)S(1)} %bitcast.114), kind=kOutput, calls=%fused_computation.13 | convolution fusion | flops 1076101120 | bytes 8388608 | tf_op jit(solution)/shard_map/dot_general | solution.py:88
  164.1 3.8 %multiply_convert_fusion = bf16[1024,2560]{1,0:T(8,128)(2,1)} fusion(bf16[1024,128]{1,0:T(8,128)(2,1)S(1)} %get-tuple-element.31, f32[1024]{0:T(1024)S(1)} %get-tuple-element.32, bf16[128,4096]{1,0:T(8,128)(2,1)S(1)} %bitcast.122), kind=kOutput, calls=%fused_computation | convolution fusion | flops 676331520 | bytes 6164480 | tf_op jit(solution)/shard_map/dot_general | solution.py:88
  172.3 3.4 %collective-permute-start.9 = (bf16[256,768]{1,0:T(8,128)(2,1)S(1)}, bf16[256,768]{1,0:T(8,128)(2,1)S(1)}, u32[]{:S(2)}, u32[]{:S(2)}) collective-permute-start(bf16[256,768]{1,0:T(8,128)(2,1)S(1)} %fusion.8), channel_id=1, source_target_pairs={{0,16},{16,32},{32,48},{48,0},{1,17},{17,33},{33,49},{49,1},{2,18}... | collective-permute-start | bytes 1179656 | tf_op jit(solution)/shard_map/ppermute | solution.py:138
  176.0 3.1 %collective-permute-start.8 = (bf16[256,768]{1,0:T(8,128)(2,1)S(1)}, bf16[256,768]{1,0:T(8,128)(2,1)S(1)}, u32[]{:S(2)}, u32[]{:S(2)}) collective-permute-start(bf16[256,768]{1,0:T(8,128)(2,1)S(1)} %fusion.7), channel_id=1, source_target_pairs={{0,48},{16,0},{32,16},{48,32},{1,49},{17,1},{33,17},{49,33},{2,50}... | collective-permute-start | bytes 1179656 | tf_op jit(solution)/shard_map/ppermute | solution.py:139
  179.3 2.3 collective-permute-start.6
  182.2 4.3 %collective-permute-start.11 = (bf16[256,768]{1,0:T(8,128)(2,1)S(1)}, bf16[256,768]{1,0:T(8,128)(2,1)S(1)}, u32[]{:S(2)}, u32[]{:S(2)}) collective-permute-start(bf16[256,768]{1,0:T(8,128)(2,1)S(1)} %add_convert_fusion.1), channel_id=1, source_target_pairs={{0,48},{16,0},{32,16},{48,32},{1,49},{17,1},{33,17},{49,33},{2,50}... | collective-permute-start | bytes 1179656 | tf_op jit(solution)/shard_map/ppermute | solution.py:141
  186.6 7.1 %collective-permute-done.6 = bf16[256,768]{1,0:T(8,128)(2,1)S(1)} collective-permute-done((bf16[256,768]{1,0:T(8,128)(2,1)S(1)}, bf16[256,768]{1,0:T(8,128)(2,1)S(1)}, u32[]{:S(2)}, u32[]{:S(2)}) %collective-permute-start.6) | collective-permute-done | bytes 393248 | tf_op jit(solution)/shard_map/ppermute | solution.py:136
  198.1 7.8 %collective-permute-done.7 = bf16[256,768]{1,0:T(8,128)(2,1)S(1)} collective-permute-done((bf16[256,768]{1,0:T(8,128)(2,1)S(1)}, bf16[256,768]{1,0:T(8,128)(2,1)S(1)}, u32[]{:S(2)}, u32[]{:S(2)}) %collective-permute-start.7) | collective-permute-done | bytes 393248 | tf_op jit(solution)/shard_map/ppermute | solution.py:140
  206.1 28.2 %all_to_all.55 = bf16[16,16,1536]{2,1,0:T(8,128)(2,1)S(1)} all-to-all(bf16[16,16,1536]{2,1,0:T(8,128)(2,1)S(1)} %bitcast.133), channel_id=1, replica_groups=mesh['group'=16,'x'=4,'z'=16] {'group'}, dimensions={0} | all-to-all | bytes 1572864 | tf_op jit(solution)/shard_map/all_to_all | solution.py:149
  235.4 4.6 %all-to-all-start.4 = ((bf16[16,4,1536]{2,1,0:T(4,128)(2,1)}), bf16[16,4,1536]{2,1,0:T(4,128)(2,1)S(1)}, u32[]{:S(2)}, u32[]{:S(2)}) async-start(bf16[16,4,1536]{2,1,0:T(4,128)(2,1)} %all_to_all.47), calls=%async_computation.5 | async-start | bytes 393216 | tf_op jit(solution)/shard_map/all_to_all | solution.py:153
  242.6 11.8 %all-to-all-done.4 = bf16[16,4,1536]{2,1,0:T(4,128)(2,1)S(1)} async-done(((bf16[16,4,1536]{2,1,0:T(4,128)(2,1)}), bf16[16,4,1536]{2,1,0:T(4,128)(2,1)S(1)}, u32[]{:S(2)}, u32[]{:S(2)}) %all-to-all-start.4) | async-done | bytes 196640 | tf_op jit(solution)/shard_map/all_to_all | solution.py:153
  254.4 5.8 %all-to-all-start.2 = ((bf16[64,2,1280]{2,1,0:T(2,128)(2,1)}), bf16[64,2,1280]{2,1,0:T(2,128)(2,1)S(1)}, u32[]{:S(2)}, u32[]{:S(2)}) async-start(bf16[64,2,1280]{2,1,0:T(2,128)(2,1)} %reshape.161), calls=%async_computation.3 | async-start | bytes 655360 | tf_op jit(solution)/shard_map/all_to_all | solution.py:155
  260.4 13.1 %all-to-all-done.2 = bf16[64,2,1280]{2,1,0:T(2,128)(2,1)S(1)} async-done(((bf16[64,2,1280]{2,1,0:T(2,128)(2,1)}), bf16[64,2,1280]{2,1,0:T(2,128)(2,1)S(1)}, u32[]{:S(2)}, u32[]{:S(2)}) %all-to-all-start.2) | async-done | bytes 327712 | tf_op jit(solution)/shard_map/all_to_all | solution.py:155
  (104 shorter events, 36.4 us)
Async XLA Ops:
  12.5 48.8 %all-to-all-start = ((bf16[64,2,1088]{2,1,0:T(2,128)(2,1)}), bf16[64,2,1088]{2,1,0:T(2,128)(2,1)S(1)}, u32[]{:S(2)}, u32[]{:S(2)}) async-start(bf16[64,2,1088]{2,1,0:T(2,128)(2,1)} %reshape.159), calls=%async_computation | async-start | bytes 589824 | tf_op jit(solution)/shard_map/all_to_all | solution.py:54
  30.8 128.2 %all-gather.3.cloned.1.call-start = ((), (), s32[]{:S(2)}) async-start(), calls=%async_computation.6 | async-start | bytes 4734976 | tf_op jit(solution)/shard_map/all_gather | solution.py:62
  62.5 177.5 %reduce-scatter.2.cloned.1.call-start = ((), (), s32[]{:S(2)}) async-start(), calls=%async_computation.7 | async-start | bytes 5570560 | tf_op jit(solution)/shard_map/reduce_scatter | solution.py:114
  63.1 49.1 %copy-start = (bf16[1,4096,128]{2,1,0:T(8,128)(2,1)S(1)}, bf16[1,4096,128]{2,1,0:T(8,128)(2,1)}, u32[]{:S(2)}) copy-start(bf16[1,4096,128]{2,1,0:T(8,128)(2,1)} %param.10) | copy-start | bytes 3145732
  63.1 49.1 %copy-start.1 = (bf16[1,4096,128]{2,1,0:T(8,128)(2,1)S(1)}, bf16[1,4096,128]{2,1,0:T(8,128)(2,1)}, u32[]{:S(2)}) copy-start(bf16[1,4096,128]{2,1,0:T(8,128)(2,1)} %param.9) | copy-start | bytes 3145732
  105.9 1.0 copy-start.3
  107.9 16.3 %collective-permute-start.1 = (bf16[256,1024]{1,0:T(8,128)(2,1)}, bf16[256,1024]{1,0:T(8,128)(2,1)S(1)}, u32[]{:S(2)}, u32[]{:S(2)}) collective-permute-start(bf16[256,1024]{1,0:T(8,128)(2,1)} %get-tuple-element.24), channel_id=1, source_target_pairs={{0,48},{16,0},{32,16},{48,32},{1,49},{17,1},{33,17},{49,33},{2,50}... | collective-permute-start | bytes 1572872 | tf_op jit(solution)/shard_map/ppermute | solution.py:77
  112.3 17.5 %collective-permute-start.5 = (bf16[256,1024]{1,0:T(8,128)(2,1)}, bf16[256,1024]{1,0:T(8,128)(2,1)}, u32[]{:S(2)}, u32[]{:S(2)}) collective-permute-start(bf16[256,1024]{1,0:T(8,128)(2,1)} %get-tuple-element.24), channel_id=1, source_target_pairs={{0,16},{16,32},{32,48},{48,0},{1,17},{17,33},{33,49},{49,1},{2,18}... | collective-permute-start | bytes 1572872 | tf_op jit(solution)/shard_map/ppermute | solution.py:78
  114.3 25.7 %collective-permute-start.2 = (bf16[256,1024]{1,0:T(8,128)(2,1)}, bf16[256,1024]{1,0:T(8,128)(2,1)S(1)}, u32[]{:S(2)}, u32[]{:S(2)}) collective-permute-start(bf16[256,1024]{1,0:T(8,128)(2,1)} %get-tuple-element.23), channel_id=1, source_target_pairs={{0,16},{16,32},{32,48},{48,0},{1,17},{17,33},{33,49},{49,1},{2,18}... | collective-permute-start | bytes 1572872 | tf_op jit(solution)/shard_map/ppermute | solution.py:76
  116.5 25.8 %collective-permute-start = (bf16[256,1024]{1,0:T(8,128)(2,1)}, bf16[256,1024]{1,0:T(8,128)(2,1)S(1)}, u32[]{:S(2)}, u32[]{:S(2)}) collective-permute-start(bf16[256,1024]{1,0:T(8,128)(2,1)} %get-tuple-element.23), channel_id=1, source_target_pairs={{0,48},{16,0},{32,16},{48,32},{1,49},{17,1},{33,17},{49,33},{2,50}... | collective-permute-start | bytes 1572872 | tf_op jit(solution)/shard_map/ppermute | solution.py:79
  124.2 21.7 %collective-permute-start.4 = (bf16[256,1024]{1,0:T(8,128)(2,1)S(1)}, bf16[256,1024]{1,0:T(8,128)(2,1)S(1)}, u32[]{:S(2)}, u32[]{:S(2)}) collective-permute-start(bf16[256,1024]{1,0:T(8,128)(2,1)S(1)} %collective-permute-done.1), channel_id=1, source_target_pairs={{0,48},{16,0},{32,16},{48,32},{1,49},{17,1},{33,17},{49,33},{2,50}... | collective-permute-start | bytes 1572872 | tf_op jit(solution)/shard_map/ppermute | solution.py:81
  140.1 16.3 %collective-permute-start.3 = (bf16[256,1024]{1,0:T(8,128)(2,1)S(1)}, bf16[256,1024]{1,0:T(8,128)(2,1)S(1)}, u32[]{:S(2)}, u32[]{:S(2)}) collective-permute-start(bf16[256,1024]{1,0:T(8,128)(2,1)S(1)} %collective-permute-done.2), channel_id=1, source_target_pairs={{0,16},{16,32},{32,48},{48,0},{1,17},{17,33},{33,49},{49,1},{2,18}... | collective-permute-start | bytes 1572872 | tf_op jit(solution)/shard_map/ppermute | solution.py:80
  159.0 5.1 %copy-start.2 = (bf16[1,128,4096]{2,1,0:T(8,128)(2,1)S(1)}, bf16[1,128,4096]{2,1,0:T(8,128)(2,1)}, u32[]{:S(2)}) copy-start(bf16[1,128,4096]{2,1,0:T(8,128)(2,1)} %param.11) | copy-start | bytes 3145732
  169.7 12.2 %collective-permute-start.10 = (bf16[256,768]{1,0:T(8,128)(2,1)S(1)}, bf16[256,768]{1,0:T(8,128)(2,1)S(1)}, u32[]{:S(2)}, u32[]{:S(2)}) collective-permute-start(bf16[256,768]{1,0:T(8,128)(2,1)S(1)} %fusion.9), channel_id=1, source_target_pairs={{0,48},{16,0},{32,16},{48,32},{1,49},{17,1},{33,17},{49,33},{2,50}... | collective-permute-start | bytes 1179656 | tf_op jit(solution)/shard_map/ppermute | solution.py:137
  172.3 23.8 %collective-permute-start.9 = (bf16[256,768]{1,0:T(8,128)(2,1)S(1)}, bf16[256,768]{1,0:T(8,128)(2,1)S(1)}, u32[]{:S(2)}, u32[]{:S(2)}) collective-permute-start(bf16[256,768]{1,0:T(8,128)(2,1)S(1)} %fusion.8), channel_id=1, source_target_pairs={{0,16},{16,32},{32,48},{48,0},{1,17},{17,33},{33,49},{49,1},{2,18}... | collective-permute-start | bytes 1179656 | tf_op jit(solution)/shard_map/ppermute | solution.py:138
  176.0 22.1 %collective-permute-start.8 = (bf16[256,768]{1,0:T(8,128)(2,1)S(1)}, bf16[256,768]{1,0:T(8,128)(2,1)S(1)}, u32[]{:S(2)}, u32[]{:S(2)}) collective-permute-start(bf16[256,768]{1,0:T(8,128)(2,1)S(1)} %fusion.7), channel_id=1, source_target_pairs={{0,48},{16,0},{32,16},{48,32},{1,49},{17,1},{33,17},{49,33},{2,50}... | collective-permute-start | bytes 1179656 | tf_op jit(solution)/shard_map/ppermute | solution.py:139
  179.3 14.3 %collective-permute-start.6 = (bf16[256,768]{1,0:T(8,128)(2,1)S(1)}, bf16[256,768]{1,0:T(8,128)(2,1)S(1)}, u32[]{:S(2)}, u32[]{:S(2)}) collective-permute-start(bf16[256,768]{1,0:T(8,128)(2,1)S(1)} %fusion.6), channel_id=1, source_target_pairs={{0,16},{16,32},{32,48},{48,0},{1,17},{17,33},{33,49},{49,1},{2,18}... | collective-permute-start | bytes 1179656 | tf_op jit(solution)/shard_map/ppermute | solution.py:136
  182.2 15.7 %collective-permute-start.11 = (bf16[256,768]{1,0:T(8,128)(2,1)S(1)}, bf16[256,768]{1,0:T(8,128)(2,1)S(1)}, u32[]{:S(2)}, u32[]{:S(2)}) collective-permute-start(bf16[256,768]{1,0:T(8,128)(2,1)S(1)} %add_convert_fusion.1), channel_id=1, source_target_pairs={{0,48},{16,0},{32,16},{48,32},{1,49},{17,1},{33,17},{49,33},{2,50}... | collective-permute-start | bytes 1179656 | tf_op jit(solution)/shard_map/ppermute | solution.py:141
  193.9 12.0 %collective-permute-start.7 = (bf16[256,768]{1,0:T(8,128)(2,1)S(1)}, bf16[256,768]{1,0:T(8,128)(2,1)S(1)}, u32[]{:S(2)}, u32[]{:S(2)}) collective-permute-start(bf16[256,768]{1,0:T(8,128)(2,1)S(1)} %add_convert_fusion.3), channel_id=1, source_target_pairs={{0,16},{16,32},{32,48},{48,0},{1,17},{17,33},{33,49},{49,1},{2,18}... | collective-permute-start | bytes 1179656 | tf_op jit(solution)/shard_map/ppermute | solution.py:140
  235.4 19.0 %all-to-all-start.4 = ((bf16[16,4,1536]{2,1,0:T(4,128)(2,1)}), bf16[16,4,1536]{2,1,0:T(4,128)(2,1)S(1)}, u32[]{:S(2)}, u32[]{:S(2)}) async-start(bf16[16,4,1536]{2,1,0:T(4,128)(2,1)} %all_to_all.47), calls=%async_computation.5 | async-start | bytes 393216 | tf_op jit(solution)/shard_map/all_to_all | solution.py:153
  254.4 19.2 %all-to-all-start.2 = ((bf16[64,2,1280]{2,1,0:T(2,128)(2,1)}), bf16[64,2,1280]{2,1,0:T(2,128)(2,1)S(1)}, u32[]{:S(2)}, u32[]{:S(2)}) async-start(bf16[64,2,1280]{2,1,0:T(2,128)(2,1)} %reshape.161), calls=%async_computation.3 | async-start | bytes 655360 | tf_op jit(solution)/shard_map/all_to_all | solution.py:155
Sparse Core Ops, SparseCore 0:
  62.6 73.7 all-gather.2
  168.0 64.1 reduce-scatter.1

commit v5 on v4

--- a/solution.py
+++ b/solution.py
@@ -6,8 +6,8 @@
 EXP_GROUP = 8
 LANES = 128
 X_CHIPS = 4
-FRONT = 2048
-FRONT_OUT = 2560
+FRONT = 2560
+FRONT_OUT = 2816
 
 
 def on_device(tokens, expert_ids, gates, gate_weight, up_weight, down_weight):
@@ -50,7 +50,10 @@
         groups * nx, FRONT + LANES
     )
     back_row, front_send = lax.optimization_barrier((back_row, front_send))
-    column = lax.all_gather(back_row, "z", axis=0, tiled=True)
+    copies = jnp.broadcast_to(back_row[None], (nz,) + back_row.shape).reshape(
+        nz * back_row.shape[0], back_row.shape[1]
+    )
+    column = lax.all_to_all(copies, "z", split_axis=0, concat_axis=0, tiled=True)
     front = lax.all_to_all(
         front_send,
         ("group", "x"),
@@ -58,7 +61,6 @@
         concat_axis=0,
         tiled=True,
     )
-    front, column = lax.optimization_barrier((front, column))
     front_all = lax.all_gather(front, "z", axis=0, tiled=True)
     tok_rows = tokens.shape[0]
     same_z = (

time: 283 us -> 272 us (0.961)
  blocking collectives: 101 us -> 56.4 us
  starting transfers between devices: 65.6 us -> 84.3 us
  waiting for transfers between devices: 65.7 us -> 83.9 us
    all_to_all x1 -> x2, waiting for transfers between devices: 0.01 us -> 35 us  [the longest x1 22.6 us: on_device(): lax.all_to_all(back, 'group', split_axis=0, concat_axis=0, tiled=True)]
    all_gather x1 -> x0, blocking collectives: 30.5 us -> none  [on_device(): column = lax.all_gather(back_row, 'z', axis=0, tiled=True)]
    all_to_all x1, starting transfers between devices: 5.78 us -> 18.5 us  [on_device(): lax.all_to_all(front_z, ('group', 'x'), split_axis=0, concat_axis=0, tile...]
    all_to_all x1, blocking collectives: 42.7 us -> 31.5 us  [on_device(): lax.all_to_all(front_send, ('group', 'x'), split_axis=0, concat_axis=0, t...]
    ppermute x1, waiting for transfers between devices: 8.86 us -> 0.36 us  [on_device(): left_low = lax.ppermute(own_low, 'x', to_right)]
    ppermute x1, waiting for transfers between devices: 7.79 us -> 0.01 us  [on_device(): lax.ppermute(part(h_right, s_right, down_low, low_in), 'x', to_right)]
    ppermute x1, waiting for transfers between devices: 7.08 us -> 0.01 us  [on_device(): low_in = lax.ppermute(part(h_far, s_far, down_low), 'x', to_right)]
    ppermute x1, waiting for transfers between devices: 10.2 us -> 3.22 us  [on_device(): far_low = lax.ppermute(left_low, 'x', to_right)]
  transfers between devices with their start and end apart: 17 -> 18, of which waited for: 9 -> 12; matrix products, arithmetic and copies ran while one was open for 6% -> 5% of each run, Pallas kernels for 0% -> 0%
where the time goes in v5:
time: 272 us; the launch traced here: 271 us
  starting transfers between devices  84.3 us (31%)
  waiting for transfers between devices  83.9 us (31%)
  blocking collectives  56.4 us (21%)
  matrix products  15 us (6%)
  between operations  14.1 us (5%)
  local copies, waits for them, and re-layouts  10 us (4%)
  other arithmetic  6.86 us (3%)
    all_to_all x1, blocking collectives, on_device(): lax.all_to_all(front_send, ('group', 'x'), split_axis=0, concat_axis=0, t...  31.5 us
    all_to_all x1, blocking collectives, on_device(): lax.all_to_all(back_out, 'group', split_axis=0, concat_axis=0, tiled=True)  24.9 us
    all_to_all x1, waiting for transfers between devices, on_device(): lax.all_to_all(back, 'group', split_axis=0, concat_axis=0, tiled=True)  22.6 us
    all_to_all x1, starting transfers between devices, on_device(): lax.all_to_all(front_z, ('group', 'x'), split_axis=0, concat_axis=0, tile...  18.5 us
    all_to_all x1, waiting for transfers between devices, on_device(): lax.all_to_all(front_z, ('group', 'x'), split_axis=0, concat_axis=0, tile...  13.7 us
    dot_general x18, matrix products, dot(): return jnp.dot(a, b, preferred_element_type=jnp.float32)  12.5 us
    all_to_all x1, starting transfers between devices, on_device(): lax.all_to_all(copies, 'z', split_axis=0, concat_axis=0, tiled=True)  12.5 us
    all_to_all x1, waiting for transfers between devices, on_device(): lax.all_to_all(copies, 'z', split_axis=0, concat_axis=0, tiled=True)  12.4 us
  transfers between devices with their start and end apart: 18, of which 12 were waited for; matrix products, arithmetic and copies ran while one was open for 5% of the time, Pallas kernels for 0%

profile of v5, /device:TPU:1, one launch (start us, length us, event | category | flops | bytes accessed | tf_op | source)
XLA Modules:
  0.0 270.6 jit_solution(1930433445373033113)
XLA Ops:
  12.0 31.5 %all_to_all.63 = bf16[64,2,1344]{2,1,0:T(2,128)(2,1)S(1)} all-to-all(bf16[64,2,1344]{2,1,0:T(2,128)(2,1)S(1)} %reshape.163), channel_id=1, replica_groups=mesh['group'=16,'x'=4,'z'=16] {'group','x'}, dimensions={0} | all-to-all | bytes 688128 | tf_op jit(solution)/shard_map/all_to_all | solution.py:57
  45.5 12.5 %all-to-all-start.1 = ((bf16[16,4,1664]{2,1,0:T(4,128)(2,1)}), bf16[16,4,1664]{2,1,0:T(4,128)(2,1)S(1)}, u32[]{:S(2)}, u32[]{:S(2)}) async-start(bf16[16,4,1664]{2,1,0:T(4,128)(2,1)} %broadcast_in_dim.8), calls=%async_computation.1 | async-start | bytes 425984 | tf_op jit(solution)/shard_map/all_to_all | solution.py:56
  58.0 12.4 %all-to-all-done.1 = bf16[16,4,1664]{2,1,0:T(4,128)(2,1)S(1)} async-done(((bf16[16,4,1664]{2,1,0:T(4,128)(2,1)}), bf16[16,4,1664]{2,1,0:T(4,128)(2,1)S(1)}, u32[]{:S(2)}, u32[]{:S(2)}) %all-to-all-start.1) | async-done | bytes 213024 | tf_op jit(solution)/shard_map/all_to_all | solution.py:56
  71.9 10.8 %all-to-all-start.2 = ((bf16[16,16,1536]{2,1,0:T(8,128)(2,1)}), bf16[16,16,1536]{2,1,0:T(8,128)(2,1)S(1)}, u32[]{:S(2)}, u32[]{:S(2)}) async-start(bf16[16,16,1536]{2,1,0:T(8,128)(2,1)} %bitcast.129), calls=%async_computation.2 | async-start | bytes 1572864 | tf_op jit(solution)/shard_map/all_to_all | solution.py:76
  82.8 22.6 %all-to-all-done.2 = bf16[16,16,1536]{2,1,0:T(8,128)(2,1)S(1)} async-done(((bf16[16,16,1536]{2,1,0:T(8,128)(2,1)}), bf16[16,16,1536]{2,1,0:T(8,128)(2,1)S(1)}, u32[]{:S(2)}, u32[]{:S(2)}) %all-to-all-start.2) | async-done | bytes 786464 | tf_op jit(solution)/shard_map/all_to_all | solution.py:76
  107.7 3.0 %collective-permute-start.2 = (bf16[256,768]{1,0:T(8,128)(2,1)S(1)}, bf16[256,768]{1,0:T(8,128)(2,1)S(1)}, u32[]{:S(2)}, u32[]{:S(2)}) collective-permute-start(bf16[256,768]{1,0:T(8,128)(2,1)S(1)} %get-tuple-element.19), channel_id=1, source_target_pairs={{0,16},{16,32},{32,48},{48,0},{1,17},{17,33},{33,49},{49,1},{2,18}... | collective-permute-start | bytes 1179656 | tf_op jit(solution)/shard_map/ppermute | solution.py:78
  110.8 3.5 %collective-permute-start = (bf16[256,768]{1,0:T(8,128)(2,1)S(1)}, bf16[256,768]{1,0:T(8,128)(2,1)S(1)}, u32[]{:S(2)}, u32[]{:S(2)}) collective-permute-start(bf16[256,768]{1,0:T(8,128)(2,1)S(1)} %get-tuple-element.19), channel_id=1, source_target_pairs={{0,48},{16,0},{32,16},{48,32},{1,49},{17,1},{33,17},{49,33},{2,50}... | collective-permute-start | bytes 1179656 | tf_op jit(solution)/shard_map/ppermute | solution.py:81
  118.6 3.1 %collective-permute-start.4 = (bf16[256,768]{1,0:T(8,128)(2,1)S(1)}, bf16[256,768]{1,0:T(8,128)(2,1)S(1)}, u32[]{:S(2)}, u32[]{:S(2)}) collective-permute-start(bf16[256,768]{1,0:T(8,128)(2,1)S(1)} %collective-permute-done.1), channel_id=1, source_target_pairs={{0,48},{16,0},{32,16},{48,32},{1,49},{17,1},{33,17},{49,33},{2,50}... | collective-permute-start | bytes 1179656 | tf_op jit(solution)/shard_map/ppermute | solution.py:83
  124.3 6.2 %collective-permute-done.5 = bf16[256,768]{1,0:T(8,128)(2,1)S(1)} collective-permute-done((bf16[256,768]{1,0:T(8,128)(2,1)S(1)}, bf16[256,768]{1,0:T(8,128)(2,1)S(1)}, u32[]{:S(2)}, u32[]{:S(2)}) %collective-permute-start.5) | collective-permute-done | bytes 393248 | tf_op jit(solution)/shard_map/ppermute | solution.py:80
  131.4 2.5 collective-permute-done.4
  134.2 3.2 %collective-permute-done.3 = bf16[256,768]{1,0:T(8,128)(2,1)S(1)} collective-permute-done((bf16[256,768]{1,0:T(8,128)(2,1)S(1)}, bf16[256,768]{1,0:T(8,128)(2,1)S(1)}, u32[]{:S(2)}, u32[]{:S(2)}) %collective-permute-start.3) | collective-permute-done | bytes 393248 | tf_op jit(solution)/shard_map/ppermute | solution.py:82
  140.0 4.4 %fusion.3 = f32[1024,256]{1,0:T(8,128)S(1)} fusion(f32[1024,256]{1,0:T(8,128)} %reshape.150, bf16[1024,2688]{1,0:T(8,128)(2,1)} %bitcast.149, bf16[4096,128]{1,0:T(8,128)(2,1)S(1)} %bitcast.117, bf16[4096,128]{1,0:T(8,128)(2,1)S(1)} %bitcast.111), kind=kOutput, calls=%fused_computation.13 | convolution fusion | flops 1345060864 | bytes 9437184 | tf_op jit(solution)/shard_map/dot_general | solution.py:90
  145.6 4.2 %multiply_convert_fusion = bf16[1024,2816]{1,0:T(8,128)(2,1)} fusion(bf16[1024,128]{1,0:T(8,128)(2,1)S(1)} %get-tuple-element.27, f32[1024]{0:T(1024)S(1)} %get-tuple-element.28, bf16[128,4096]{1,0:T(8,128)(2,1)S(1)} %bitcast.120), kind=kOutput, calls=%fused_computation | convolution fusion | flops 743964672 | bytes 6754304 | tf_op jit(solution)/shard_map/dot_general | solution.py:90
  154.0 4.6 %collective-permute-start.8 = (bf16[256,640]{1,0:T(8,128)(2,1)S(1)}, bf16[256,640]{1,0:T(8,128)(2,1)S(1)}, u32[]{:S(2)}, u32[]{:S(2)}) collective-permute-start(bf16[256,640]{1,0:T(8,128)(2,1)S(1)} %fusion.9), channel_id=1, source_target_pairs={{0,48},{16,0},{32,16},{48,32},{1,49},{17,1},{33,17},{49,33},{2,50}... | collective-permute-start | bytes 983048 | tf_op jit(solution)/shard_map/ppermute | solution.py:141
  161.3 4.6 %collective-permute-start.10 = (bf16[256,640]{1,0:T(8,128)(2,1)S(1)}, bf16[256,640]{1,0:T(8,128)(2,1)S(1)}, u32[]{:S(2)}, u32[]{:S(2)}) collective-permute-start(bf16[256,640]{1,0:T(8,128)(2,1)S(1)} %fusion.11), channel_id=1, source_target_pairs={{0,48},{16,0},{32,16},{48,32},{1,49},{17,1},{33,17},{49,33},{2,50}... | collective-permute-start | bytes 983048 | tf_op jit(solution)/shard_map/ppermute | solution.py:139
  168.4 4.3 %collective-permute-done.10 = bf16[256,640]{1,0:T(8,128)(2,1)S(1)} collective-permute-done((bf16[256,640]{1,0:T(8,128)(2,1)S(1)}, bf16[256,640]{1,0:T(8,128)(2,1)S(1)}, u32[]{:S(2)}, u32[]{:S(2)}) %collective-permute-start.10) | collective-permute-done | bytes 327712 | tf_op jit(solution)/shard_map/ppermute | solution.py:139
  172.9 5.3 %collective-permute-start.11 = (bf16[256,640]{1,0:T(8,128)(2,1)S(1)}, bf16[256,640]{1,0:T(8,128)(2,1)S(1)}, u32[]{:S(2)}, u32[]{:S(2)}) collective-permute-start(bf16[256,640]{1,0:T(8,128)(2,1)S(1)} %add_convert_fusion.1), channel_id=1, source_target_pairs={{0,48},{16,0},{32,16},{48,32},{1,49},{17,1},{33,17},{49,33},{2,50}... | collective-permute-start | bytes 983048 | tf_op jit(solution)/shard_map/ppermute | solution.py:143
  178.6 5.4 %collective-permute-done.11 = bf16[256,640]{1,0:T(8,128)(2,1)S(1)} collective-permute-done((bf16[256,640]{1,0:T(8,128)(2,1)S(1)}, bf16[256,640]{1,0:T(8,128)(2,1)S(1)}, u32[]{:S(2)}, u32[]{:S(2)}) %collective-permute-start.11) | collective-permute-done | bytes 327712 | tf_op jit(solution)/shard_map/ppermute | solution.py:143
  184.2 24.9 %all_to_all.64 = bf16[16,16,1280]{2,1,0:T(8,128)(2,1)S(1)} all-to-all(bf16[16,16,1280]{2,1,0:T(8,128)(2,1)S(1)} %bitcast.130), channel_id=1, replica_groups=mesh['group'=16,'x'=4,'z'=16] {'group'}, dimensions={0} | all-to-all | bytes 1310720 | tf_op jit(solution)/shard_map/all_to_all | solution.py:151
  210.1 6.4 %all-to-all-start.5 = ((bf16[16,4,1280]{2,1,0:T(4,128)(2,1)}), bf16[16,4,1280]{2,1,0:T(4,128)(2,1)S(1)}, u32[]{:S(2)}, u32[]{:S(2)}) async-start(bf16[16,4,1280]{2,1,0:T(4,128)(2,1)} %all_to_all.55), calls=%async_computation.6 | async-start | bytes 327680 | tf_op jit(solution)/shard_map/all_to_all | solution.py:155
  216.5 4.1 %reduce-scatter.2.cloned.1.call-done = bf16[64,2816]{1,0:T(8,128)(2,1)} async-done(((bf16[1024,2816]{1,0:T(8,128)(2,1)}), bf16[64,2816]{1,0:T(8,128)(2,1)}) %reduce-scatter.2.cloned.1.call-update) | async-done | bytes 360464 | tf_op jit(solution)/shard_map/reduce_scatter | solution.py:116
  223.3 6.9 %all-to-all-done.5 = bf16[16,4,1280]{2,1,0:T(4,128)(2,1)S(1)} async-done(((bf16[16,4,1280]{2,1,0:T(4,128)(2,1)}), bf16[16,4,1280]{2,1,0:T(4,128)(2,1)S(1)}, u32[]{:S(2)}, u32[]{:S(2)}) %all-to-all-start.5) | async-done | bytes 163872 | tf_op jit(solution)/shard_map/all_to_all | solution.py:155
  230.2 18.5 %all-to-all-start.3 = ((bf16[64,2,1408]{2,1,0:T(2,128)(2,1)}), bf16[64,2,1408]{2,1,0:T(2,128)(2,1)S(1)}, u32[]{:S(2)}, u32[]{:S(2)}) async-start(bf16[64,2,1408]{2,1,0:T(2,128)(2,1)} %reshape.165), calls=%async_computation.4 | async-start | bytes 720896 | tf_op jit(solution)/shard_map/all_to_all | solution.py:157
  249.0 13.7 %all-to-all-done.3 = bf16[64,2,1408]{2,1,0:T(2,128)(2,1)S(1)} async-done(((bf16[64,2,1408]{2,1,0:T(2,128)(2,1)}), bf16[64,2,1408]{2,1,0:T(2,128)(2,1)S(1)}, u32[]{:S(2)}, u32[]{:S(2)}) %all-to-all-start.3) | async-done | bytes 360480 | tf_op jit(solution)/shard_map/all_to_all | solution.py:157
  (104 shorter events, 37.9 us)
Async XLA Ops:
  6.5 133.4 %all-gather.3.cloned.1.call-start = ((), (), s32[]{:S(2)}) async-start(), calls=%async_computation.8 | async-start | bytes 5849088 | tf_op jit(solution)/shard_map/all_gather | solution.py:64
  45.5 24.9 %all-to-all-start.1 = ((bf16[16,4,1664]{2,1,0:T(4,128)(2,1)}), bf16[16,4,1664]{2,1,0:T(4,128)(2,1)S(1)}, u32[]{:S(2)}, u32[]{:S(2)}) async-start(bf16[16,4,1664]{2,1,0:T(4,128)(2,1)} %broadcast_in_dim.8), calls=%async_computation.1 | async-start | bytes 425984 | tf_op jit(solution)/shard_map/all_to_all | solution.py:56
  70.7 40.1 %copy-start = (bf16[1,4096,128]{2,1,0:T(8,128)(2,1)S(1)}, bf16[1,4096,128]{2,1,0:T(8,128)(2,1)}, u32[]{:S(2)}) copy-start(bf16[1,4096,128]{2,1,0:T(8,128)(2,1)} %param.10) | copy-start | bytes 3145732
  70.7 40.1 %copy-start.1 = (bf16[1,4096,128]{2,1,0:T(8,128)(2,1)S(1)}, bf16[1,4096,128]{2,1,0:T(8,128)(2,1)}, u32[]{:S(2)}) copy-start(bf16[1,4096,128]{2,1,0:T(8,128)(2,1)} %param.9) | copy-start | bytes 3145732
  71.9 33.5 %all-to-all-start.2 = ((bf16[16,16,1536]{2,1,0:T(8,128)(2,1)}), bf16[16,16,1536]{2,1,0:T(8,128)(2,1)S(1)}, u32[]{:S(2)}, u32[]{:S(2)}) async-start(bf16[16,16,1536]{2,1,0:T(8,128)(2,1)} %bitcast.129), calls=%async_computation.2 | async-start | bytes 1572864 | tf_op jit(solution)/shard_map/all_to_all | solution.py:76
  82.7 137.9 %reduce-scatter.2.cloned.1.call-start = ((), (), s32[]{:S(2)}) async-start(), calls=%async_computation.7 | async-start | bytes 6127616 | tf_op jit(solution)/shard_map/reduce_scatter | solution.py:116
  105.4 13.2 %collective-permute-start.1 = (bf16[256,768]{1,0:T(8,128)(2,1)S(1)}, bf16[256,768]{1,0:T(8,128)(2,1)S(1)}, u32[]{:S(2)}, u32[]{:S(2)}) collective-permute-start(bf16[256,768]{1,0:T(8,128)(2,1)S(1)} %get-tuple-element.20), channel_id=1, source_target_pairs={{0,48},{16,0},{32,16},{48,32},{1,49},{17,1},{33,17},{49,33},{2,50}... | collective-permute-start | bytes 1179656 | tf_op jit(solution)/shard_map/ppermute | solution.py:79
  107.7 14.4 %collective-permute-start.2 = (bf16[256,768]{1,0:T(8,128)(2,1)S(1)}, bf16[256,768]{1,0:T(8,128)(2,1)S(1)}, u32[]{:S(2)}, u32[]{:S(2)}) collective-permute-start(bf16[256,768]{1,0:T(8,128)(2,1)S(1)} %get-tuple-element.19), channel_id=1, source_target_pairs={{0,16},{16,32},{32,48},{48,0},{1,17},{17,33},{33,49},{49,1},{2,18}... | collective-permute-start | bytes 1179656 | tf_op jit(solution)/shard_map/ppermute | solution.py:78
  110.8 20.3 %collective-permute-start = (bf16[256,768]{1,0:T(8,128)(2,1)S(1)}, bf16[256,768]{1,0:T(8,128)(2,1)S(1)}, u32[]{:S(2)}, u32[]{:S(2)}) collective-permute-start(bf16[256,768]{1,0:T(8,128)(2,1)S(1)} %get-tuple-element.19), channel_id=1, source_target_pairs={{0,48},{16,0},{32,16},{48,32},{1,49},{17,1},{33,17},{49,33},{2,50}... | collective-permute-start | bytes 1179656 | tf_op jit(solution)/shard_map/ppermute | solution.py:81
  114.3 16.2 %collective-permute-start.5 = (bf16[256,768]{1,0:T(8,128)(2,1)S(1)}, bf16[256,768]{1,0:T(8,128)(2,1)S(1)}, u32[]{:S(2)}, u32[]{:S(2)}) collective-permute-start(bf16[256,768]{1,0:T(8,128)(2,1)S(1)} %get-tuple-element.20), channel_id=1, source_target_pairs={{0,16},{16,32},{32,48},{48,0},{1,17},{17,33},{33,49},{49,1},{2,18}... | collective-permute-start | bytes 1179656 | tf_op jit(solution)/shard_map/ppermute | solution.py:80
  118.6 15.3 %collective-permute-start.4 = (bf16[256,768]{1,0:T(8,128)(2,1)S(1)}, bf16[256,768]{1,0:T(8,128)(2,1)S(1)}, u32[]{:S(2)}, u32[]{:S(2)}) collective-permute-start(bf16[256,768]{1,0:T(8,128)(2,1)S(1)} %collective-permute-done.1), channel_id=1, source_target_pairs={{0,48},{16,0},{32,16},{48,32},{1,49},{17,1},{33,17},{49,33},{2,50}... | collective-permute-start | bytes 1179656 | tf_op jit(solution)/shard_map/ppermute | solution.py:83
  122.1 15.3 %collective-permute-start.3 = (bf16[256,768]{1,0:T(8,128)(2,1)S(1)}, bf16[256,768]{1,0:T(8,128)(2,1)S(1)}, u32[]{:S(2)}, u32[]{:S(2)}) collective-permute-start(bf16[256,768]{1,0:T(8,128)(2,1)S(1)} %collective-permute-done.2), channel_id=1, source_target_pairs={{0,16},{16,32},{32,48},{48,0},{1,17},{17,33},{33,49},{49,1},{2,18}... | collective-permute-start | bytes 1179656 | tf_op jit(solution)/shard_map/ppermute | solution.py:82
  140.0 5.6 %copy-start.2 = (bf16[1,128,4096]{2,1,0:T(8,128)(2,1)S(1)}, bf16[1,128,4096]{2,1,0:T(8,128)(2,1)}, u32[]{:S(2)}) copy-start(bf16[1,128,4096]{2,1,0:T(8,128)(2,1)} %param.11) | copy-start | bytes 3145732
  151.4 14.8 %collective-permute-start.6 = (bf16[256,640]{1,0:T(8,128)(2,1)S(1)}, bf16[256,640]{1,0:T(8,128)(2,1)S(1)}, u32[]{:S(2)}, u32[]{:S(2)}) collective-permute-start(bf16[256,640]{1,0:T(8,128)(2,1)S(1)} %fusion.8), channel_id=1, source_target_pairs={{0,16},{16,32},{32,48},{48,0},{1,17},{17,33},{33,49},{49,1},{2,18}... | collective-permute-start | bytes 983048 | tf_op jit(solution)/shard_map/ppermute | solution.py:138
  154.0 24.5 %collective-permute-start.8 = (bf16[256,640]{1,0:T(8,128)(2,1)S(1)}, bf16[256,640]{1,0:T(8,128)(2,1)S(1)}, u32[]{:S(2)}, u32[]{:S(2)}) collective-permute-start(bf16[256,640]{1,0:T(8,128)(2,1)S(1)} %fusion.9), channel_id=1, source_target_pairs={{0,48},{16,0},{32,16},{48,32},{1,49},{17,1},{33,17},{49,33},{2,50}... | collective-permute-start | bytes 983048 | tf_op jit(solution)/shard_map/ppermute | solution.py:141
  159.2 19.4 %collective-permute-start.9 = (bf16[256,640]{1,0:T(8,128)(2,1)S(1)}, bf16[256,640]{1,0:T(8,128)(2,1)S(1)}, u32[]{:S(2)}, u32[]{:S(2)}) collective-permute-start(bf16[256,640]{1,0:T(8,128)(2,1)S(1)} %fusion.10), channel_id=1, source_target_pairs={{0,16},{16,32},{32,48},{48,0},{1,17},{17,33},{33,49},{49,1},{2,18}... | collective-permute-start | bytes 983048 | tf_op jit(solution)/shard_map/ppermute | solution.py:140
  161.3 11.3 %collective-permute-start.10 = (bf16[256,640]{1,0:T(8,128)(2,1)S(1)}, bf16[256,640]{1,0:T(8,128)(2,1)S(1)}, u32[]{:S(2)}, u32[]{:S(2)}) collective-permute-start(bf16[256,640]{1,0:T(8,128)(2,1)S(1)} %fusion.11), channel_id=1, source_target_pairs={{0,48},{16,0},{32,16},{48,32},{1,49},{17,1},{33,17},{49,33},{2,50}... | collective-permute-start | bytes 983048 | tf_op jit(solution)/shard_map/ppermute | solution.py:139
  166.4 12.1 %collective-permute-start.7 = (bf16[256,640]{1,0:T(8,128)(2,1)S(1)}, bf16[256,640]{1,0:T(8,128)(2,1)S(1)}, u32[]{:S(2)}, u32[]{:S(2)}) collective-permute-start(bf16[256,640]{1,0:T(8,128)(2,1)S(1)} %add_convert_fusion.3), channel_id=1, source_target_pairs={{0,16},{16,32},{32,48},{48,0},{1,17},{17,33},{33,49},{49,1},{2,18}... | collective-permute-start | bytes 983048 | tf_op jit(solution)/shard_map/ppermute | solution.py:142
  172.9 11.1 %collective-permute-start.11 = (bf16[256,640]{1,0:T(8,128)(2,1)S(1)}, bf16[256,640]{1,0:T(8,128)(2,1)S(1)}, u32[]{:S(2)}, u32[]{:S(2)}) collective-permute-start(bf16[256,640]{1,0:T(8,128)(2,1)S(1)} %add_convert_fusion.1), channel_id=1, source_target_pairs={{0,48},{16,0},{32,16},{48,32},{1,49},{17,1},{33,17},{49,33},{2,50}... | collective-permute-start | bytes 983048 | tf_op jit(solution)/shard_map/ppermute | solution.py:143
  210.1 20.1 %all-to-all-start.5 = ((bf16[16,4,1280]{2,1,0:T(4,128)(2,1)}), bf16[16,4,1280]{2,1,0:T(4,128)(2,1)S(1)}, u32[]{:S(2)}, u32[]{:S(2)}) async-start(bf16[16,4,1280]{2,1,0:T(4,128)(2,1)} %all_to_all.55), calls=%async_computation.6 | async-start | bytes 327680 | tf_op jit(solution)/shard_map/all_to_all | solution.py:155
  230.2 32.5 %all-to-all-start.3 = ((bf16[64,2,1408]{2,1,0:T(2,128)(2,1)}), bf16[64,2,1408]{2,1,0:T(2,128)(2,1)S(1)}, u32[]{:S(2)}, u32[]{:S(2)}) async-start(bf16[64,2,1408]{2,1,0:T(2,128)(2,1)} %reshape.165), calls=%async_computation.4 | async-start | bytes 720896 | tf_op jit(solution)/shard_map/all_to_all | solution.py:157
Sparse Core Ops, SparseCore 0:
  44.9 82.8 all-gather.2
  149.9 70.6 reduce-scatter.1

commit v6 on v5

--- a/solution.py
+++ b/solution.py
@@ -1,13 +1,60 @@
 import jax
 import jax.numpy as jnp
 from jax import lax
+from jax.experimental import pallas as pl
+from jax.experimental.pallas import tpu as pltpu
 from jax.sharding import Mesh, PartitionSpec as P
 
 EXP_GROUP = 8
 LANES = 128
 X_CHIPS = 4
-FRONT = 2560
+FRONT = 2304
 FRONT_OUT = 2816
+
+
+ROWS = 128
+
+
+def expert_kernel(front_ref, both_ref, act_ref, own_ref, down_ref, hidden_ref, out_ref):
+    units = hidden_ref.shape[1]
+    act = act_ref[...] + jnp.dot(
+        front_ref[:, :FRONT], both_ref[...], preferred_element_type=jnp.float32
+    )
+    gate_act, up_act = act[:, :units], act[:, units:]
+    hidden = (gate_act / (1.0 + jnp.exp(-gate_act)) * up_act).astype(jnp.bfloat16)
+    hidden_ref[...] = hidden
+    table = front_ref[:, FRONT:].astype(jnp.float32)
+    scale = jnp.sum(table * own_ref[...], axis=1, keepdims=True)
+    out = jnp.dot(hidden, down_ref[...], preferred_element_type=jnp.float32)
+    out_ref[...] = (out * scale).astype(jnp.bfloat16)
+
+
+def expert_rows(front, both, act, own, down):
+    rows = front.shape[0]
+    units = down.shape[0]
+
+    def by_rows(width):
+        return pl.BlockSpec((ROWS, width), lambda i: (i, 0))
+
+    def whole(array):
+        return pl.BlockSpec(array.shape, lambda i: (0, 0))
+
+    return pl.pallas_call(
+        expert_kernel,
+        grid=(rows // ROWS,),
+        in_specs=[by_rows(front.shape[1]), whole(both), by_rows(2 * units), whole(own), whole(down)],
+        out_specs=[by_rows(units), by_rows(down.shape[1])],
+        out_shape=[
+            jax.ShapeDtypeStruct((rows, units), jnp.bfloat16),
+            jax.ShapeDtypeStruct((rows, down.shape[1]), jnp.bfloat16),
+        ],
+        compiler_params=pltpu.CompilerParams(vmem_limit_bytes=56 * 1024 * 1024),
+        cost_estimate=pl.CostEstimate(
+            flops=2 * rows * (2 * both.shape[0] + down.shape[1]) * units,
+            bytes_accessed=2 * rows * (front.shape[1] + down.shape[1]),
+            transcendentals=rows * units,
+        ),
+    )(front, both, act, own, down)
 
 
 def on_device(tokens, expert_ids, gates, gate_weight, up_weight, down_weight):
@@ -49,11 +96,11 @@
     front_send = jnp.broadcast_to(front_row[:, None], (groups, nx, FRONT + LANES)).reshape(
         groups * nx, FRONT + LANES
     )
-    back_row, front_send = lax.optimization_barrier((back_row, front_send))
     copies = jnp.broadcast_to(back_row[None], (nz,) + back_row.shape).reshape(
         nz * back_row.shape[0], back_row.shape[1]
     )
     column = lax.all_to_all(copies, "z", split_axis=0, concat_axis=0, tiled=True)
+    front_send, column = lax.optimization_barrier((front_send, column))
     front = lax.all_to_all(
         front_send,
         ("group", "x"),
@@ -105,14 +152,14 @@
         ],
         axis=2,
     ).transpose(1, 0, 2, 3).reshape(nz * groups * nx, 2 * units)
-    act = dot(front_all[:, :FRONT], both_front) + act_back
-    hidden = (jax.nn.silu(act[:, :units]) * act[:, units:]).astype(jnp.bfloat16)
     mine = (x_me * nz + lax.axis_index("z")) // slices
     own = (jnp.arange(LANES, dtype=jnp.int32) == mine).astype(jnp.float32)
     scale = jnp.sum(front_all[:, FRONT:].astype(jnp.float32) * own[None, :], axis=1, keepdims=True)
 
     down = down_weight[0]
-    front_out = (dot(hidden, down[:, :FRONT_OUT]) * scale).astype(jnp.bfloat16)
+    hidden, front_out = expert_rows(
+        front_all, both_front, act_back, own[None, :], down[:, :FRONT_OUT]
+    )
     front_z = lax.psum_scatter(front_out, "z", scatter_dimension=0, tiled=True)
     out_width = features - FRONT_OUT
     middle = FRONT_OUT + out_width // 2

time: 272 us -> 286 us (1.051)
  Pallas kernels: 0 us -> 11.5 us
  matrix products: 15 us -> 8 us
  starting transfers between devices: 84.3 us -> 88.8 us
  local copies, waits for them, and re-layouts: 10 us -> 13 us
    pallas_call x0 -> x1, Pallas kernels: none -> 11.5 us  [expert_rows(): pl.pallas_call(expert_kernel, grid=(rows // ROWS,), in_specs=[by_rows(fro...]
    reduce_scatter x1, waiting for transfers between devices: 4.11 us -> 12.9 us  [on_device(): front_z = lax.psum_scatter(front_out, 'z', scatter_dimension=0, tiled=True)]
    dot_general x18 -> x16, matrix products: 12.5 us -> 5.42 us  [dot(): return jnp.dot(a, b, preferred_element_type=jnp.float32)]
    all_to_all x1, waiting for transfers between devices: 6.95 us -> 0.01 us  [on_device(): lax.all_to_all(back_tokens, 'z', split_axis=0, concat_axis=0, tiled=True)]
    all_to_all x1, starting transfers between devices: 12.5 us -> 19.4 us  [on_device(): lax.all_to_all(copies, 'z', split_axis=0, concat_axis=0, tiled=True)]
    all_to_all x1, starting transfers between devices: 10.8 us -> 6.11 us  [on_device(): lax.all_to_all(back, 'group', split_axis=0, concat_axis=0, tiled=True)]
  transfers between devices with their start and end apart: 18 -> 18, of which waited for: 12 -> 11; matrix products, arithmetic and copies ran while one was open for 5% -> 8% of each run, Pallas kernels for 0% -> 0%
where the time goes in v6:
time: 286 us; the launch traced here: 285 us
  starting transfers between devices  88.8 us (31%)
  waiting for transfers between devices  83.3 us (29%)
  blocking collectives  56.6 us (20%)
  between operations  14.1 us (5%)
  local copies, waits for them, and re-layouts  13 us (5%)
  Pallas kernels  11.5 us (4%)
  other arithmetic  9.46 us (3%)
  matrix products  8 us (3%)
    all_to_all x1, blocking collectives, on_device(): lax.all_to_all(front_send, ('group', 'x'), split_axis=0, concat_axis=0, t...  29.1 us
    all_to_all x1, blocking collectives, on_device(): lax.all_to_all(back_out, 'group', split_axis=0, concat_axis=0, tiled=True)  27.5 us
    all_to_all x1, waiting for transfers between devices, on_device(): lax.all_to_all(back, 'group', split_axis=0, concat_axis=0, tiled=True)  23.2 us
    all_to_all x1, starting transfers between devices, on_device(): lax.all_to_all(copies, 'z', split_axis=0, concat_axis=0, tiled=True)  19.4 us
    all_to_all x1, starting transfers between devices, on_device(): lax.all_to_all(front_z, ('group', 'x'), split_axis=0, concat_axis=0, tile...  19.2 us
    all_to_all x1, waiting for transfers between devices, on_device(): lax.all_to_all(front_z, ('group', 'x'), split_axis=0, concat_axis=0, tile...  13.7 us
    reduce_scatter x1, waiting for transfers between devices, on_device(): front_z = lax.psum_scatter(front_out, 'z', scatter_dimension=0, tiled=True)  12.9 us
    pallas_call x1, Pallas kernels, expert_rows(): pl.pallas_call(expert_kernel, grid=(rows // ROWS,), in_specs=[by_rows(fro...  11.5 us
  transfers between devices with their start and end apart: 18, of which 11 were waited for; matrix products, arithmetic and copies ran while one was open for 8% of the time, Pallas kernels for 0%

profile of v6, /device:TPU:1, one launch (start us, length us, event | category | flops | bytes accessed | tf_op | source)
XLA Modules:
  0.0 284.8 jit_solution(12904070434299248481)
XLA Ops:
  8.8 19.4 %all-to-all-start = ((bf16[16,4,1920]{2,1,0:T(4,128)(2,1)}), bf16[16,4,1920]{2,1,0:T(4,128)(2,1)S(1)}, u32[]{:S(2)}, u32[]{:S(2)}) async-start(bf16[16,4,1920]{2,1,0:T(4,128)(2,1)} %broadcast_in_dim.8), calls=%async_computation | async-start | bytes 491520 | tf_op jit(solution)/shard_map/all_to_all | solution.py:102
  30.5 10.7 %all-to-all-done = bf16[16,4,1920]{2,1,0:T(4,128)(2,1)S(1)} async-done(((bf16[16,4,1920]{2,1,0:T(4,128)(2,1)}), bf16[16,4,1920]{2,1,0:T(4,128)(2,1)S(1)}, u32[]{:S(2)}, u32[]{:S(2)}) %all-to-all-start) | async-done | bytes 245792 | tf_op jit(solution)/shard_map/all_to_all | solution.py:102
  42.9 29.1 %all_to_all.63 = bf16[64,2,1216]{2,1,0:T(2,128)(2,1)S(1)} all-to-all(bf16[64,2,1216]{2,1,0:T(2,128)(2,1)S(1)} %reshape.168), channel_id=1, replica_groups=mesh['group'=16,'x'=4,'z'=16] {'group','x'}, dimensions={0} | all-to-all | bytes 622592 | tf_op jit(solution)/shard_map/all_to_all | solution.py:104
  74.7 6.1 %all-to-all-start.2 = ((bf16[16,16,1792]{2,1,0:T(8,128)(2,1)}), bf16[16,16,1792]{2,1,0:T(8,128)(2,1)}, u32[]{:S(2)}, u32[]{:S(2)}) async-start(bf16[16,16,1792]{2,1,0:T(8,128)(2,1)} %bitcast.128), calls=%async_computation.2 | async-start | bytes 1835008 | tf_op jit(solution)/shard_map/all_to_all | solution.py:123
  83.0 23.2 %all-to-all-done.2 = bf16[16,16,1792]{2,1,0:T(8,128)(2,1)} async-done(((bf16[16,16,1792]{2,1,0:T(8,128)(2,1)}), bf16[16,16,1792]{2,1,0:T(8,128)(2,1)}, u32[]{:S(2)}, u32[]{:S(2)}) %all-to-all-start.2) | async-done | bytes 917536 | tf_op jit(solution)/shard_map/all_to_all | solution.py:123
  107.5 2.7 collective-permute-start.1
  110.3 2.5 collective-permute-start.2
  113.5 4.0 %collective-permute-start = (bf16[256,896]{1,0:T(8,128)(2,1)S(1)}, bf16[256,896]{1,0:T(8,128)(2,1)S(1)}, u32[]{:S(2)}, u32[]{:S(2)}) collective-permute-start(bf16[256,896]{1,0:T(8,128)(2,1)S(1)} %get-tuple-element.23), channel_id=1, source_target_pairs={{0,48},{16,0},{32,16},{48,32},{1,49},{17,1},{33,17},{49,33},{2,50}... | collective-permute-start | bytes 1376264 | tf_op jit(solution)/shard_map/ppermute | solution.py:128
  117.4 1.9 collective-permute-start.5
  122.0 3.8 %collective-permute-start.4 = (bf16[256,896]{1,0:T(8,128)(2,1)S(1)}, bf16[256,896]{1,0:T(8,128)(2,1)S(1)}, u32[]{:S(2)}, u32[]{:S(2)}) collective-permute-start(bf16[256,896]{1,0:T(8,128)(2,1)S(1)} %collective-permute-done.1), channel_id=1, source_target_pairs={{0,48},{16,0},{32,16},{48,32},{1,49},{17,1},{33,17},{49,33},{2,50}... | collective-permute-start | bytes 1376264 | tf_op jit(solution)/shard_map/ppermute | solution.py:130
  128.2 7.6 %collective-permute-done.5 = bf16[256,896]{1,0:T(8,128)(2,1)S(1)} collective-permute-done((bf16[256,896]{1,0:T(8,128)(2,1)S(1)}, bf16[256,896]{1,0:T(8,128)(2,1)S(1)}, u32[]{:S(2)}, u32[]{:S(2)}) %collective-permute-start.5) | collective-permute-done | bytes 458784 | tf_op jit(solution)/shard_map/ppermute | solution.py:127
  136.8 3.9 %collective-permute-done.4 = bf16[256,896]{1,0:T(8,128)(2,1)S(1)} collective-permute-done((bf16[256,896]{1,0:T(8,128)(2,1)S(1)}, bf16[256,896]{1,0:T(8,128)(2,1)S(1)}, u32[]{:S(2)}, u32[]{:S(2)}) %collective-permute-start.4) | collective-permute-done | bytes 458784 | tf_op jit(solution)/shard_map/ppermute | solution.py:130
  141.0 3.7 %collective-permute-done.3 = bf16[256,896]{1,0:T(8,128)(2,1)S(1)} collective-permute-done((bf16[256,896]{1,0:T(8,128)(2,1)S(1)}, bf16[256,896]{1,0:T(8,128)(2,1)S(1)}, u32[]{:S(2)}, u32[]{:S(2)}) %collective-permute-start.3) | collective-permute-done | bytes 458784 | tf_op jit(solution)/shard_map/ppermute | solution.py:129
  147.3 11.5 %shard_map.64 = (bf16[1024,128]{1,0:T(8,128)(2,1)}, bf16[1024,2816]{1,0:T(8,128)(2,1)}) custom-call(bf16[1024,2432]{1,0:T(8,128)(2,1)} %bitcast.117, bf16[2304,256]{1,0:T(8,128)(2,1)} %fusion.5.both_ref, f32[1024,256]{1,0:T(8,128)} %reshape.155.act_ref, f32[1,128]{1,0:T(1,128)} %compare_convert_fusion.1.own_ref, bf16[128,2816]{1,0:T(8,128)(2,1)} %slice.67.down_ref), custom_call_target="tpu_custom_call" | custom-call | flops 1946157056 | bytes 10747904 | tf_op jit(solution)/shard_map/pallas_call | solution.py:42
  165.1 4.6 %collective-permute-start.8 = (bf16[256,640]{1,0:T(8,128)(2,1)S(1)}, bf16[256,640]{1,0:T(8,128)(2,1)}, u32[]{:S(2)}, u32[]{:S(2)}) collective-permute-start(bf16[256,640]{1,0:T(8,128)(2,1)S(1)} %fusion.2), channel_id=1, source_target_pairs={{0,48},{16,0},{32,16},{48,32},{1,49},{17,1},{33,17},{49,33},{2,50}... | collective-permute-start | bytes 983048 | tf_op jit(solution)/shard_map/ppermute | solution.py:188
  172.3 4.6 %collective-permute-start.10 = (bf16[256,640]{1,0:T(8,128)(2,1)S(1)}, bf16[256,640]{1,0:T(8,128)(2,1)S(1)}, u32[]{:S(2)}, u32[]{:S(2)}) collective-permute-start(bf16[256,640]{1,0:T(8,128)(2,1)S(1)} %fusion.4), channel_id=1, source_target_pairs={{0,48},{16,0},{32,16},{48,32},{1,49},{17,1},{33,17},{49,33},{2,50}... | collective-permute-start | bytes 983048 | tf_op jit(solution)/shard_map/ppermute | solution.py:186
  179.3 3.1 %collective-permute-done.10 = bf16[256,640]{1,0:T(8,128)(2,1)S(1)} collective-permute-done((bf16[256,640]{1,0:T(8,128)(2,1)S(1)}, bf16[256,640]{1,0:T(8,128)(2,1)S(1)}, u32[]{:S(2)}, u32[]{:S(2)}) %collective-permute-start.10) | collective-permute-done | bytes 327712 | tf_op jit(solution)/shard_map/ppermute | solution.py:186
  182.6 5.4 %collective-permute-start.11 = (bf16[256,640]{1,0:T(8,128)(2,1)S(1)}, bf16[256,640]{1,0:T(8,128)(2,1)S(1)}, u32[]{:S(2)}, u32[]{:S(2)}) collective-permute-start(bf16[256,640]{1,0:T(8,128)(2,1)S(1)} %add_convert_fusion.1), channel_id=1, source_target_pairs={{0,48},{16,0},{32,16},{48,32},{1,49},{17,1},{33,17},{49,33},{2,50}... | collective-permute-start | bytes 983048 | tf_op jit(solution)/shard_map/ppermute | solution.py:190
  189.3 3.3 %collective-permute-done.11 = bf16[256,640]{1,0:T(8,128)(2,1)S(1)} collective-permute-done((bf16[256,640]{1,0:T(8,128)(2,1)S(1)}, bf16[256,640]{1,0:T(8,128)(2,1)S(1)}, u32[]{:S(2)}, u32[]{:S(2)}) %collective-permute-start.11) | collective-permute-done | bytes 327712 | tf_op jit(solution)/shard_map/ppermute | solution.py:190
  192.8 27.5 %all_to_all.64 = bf16[16,16,1280]{2,1,0:T(8,128)(2,1)S(1)} all-to-all(bf16[16,16,1280]{2,1,0:T(8,128)(2,1)S(1)} %bitcast.129), channel_id=1, replica_groups=mesh['group'=16,'x'=4,'z'=16] {'group'}, dimensions={0} | all-to-all | bytes 1310720 | tf_op jit(solution)/shard_map/all_to_all | solution.py:198
  221.3 6.7 %all-to-all-start.5 = ((bf16[16,4,1280]{2,1,0:T(4,128)(2,1)}), bf16[16,4,1280]{2,1,0:T(4,128)(2,1)S(1)}, u32[]{:S(2)}, u32[]{:S(2)}) async-start(bf16[16,4,1280]{2,1,0:T(4,128)(2,1)} %all_to_all.55), calls=%async_computation.6 | async-start | bytes 327680 | tf_op jit(solution)/shard_map/all_to_all | solution.py:202
  228.0 12.9 %reduce-scatter.2.cloned.1.call-done = bf16[64,2816]{1,0:T(8,128)(2,1)} async-done(((bf16[1024,2816]{1,0:T(8,128)(2,1)}), bf16[64,2816]{1,0:T(8,128)(2,1)}) %reduce-scatter.2.cloned.1.call-update) | async-done | bytes 360464 | tf_op jit(solution)/shard_map/reduce_scatter | solution.py:163
  243.6 19.2 %all-to-all-start.3 = ((bf16[64,2,1408]{2,1,0:T(2,128)(2,1)}), bf16[64,2,1408]{2,1,0:T(2,128)(2,1)S(1)}, u32[]{:S(2)}, u32[]{:S(2)}) async-start(bf16[64,2,1408]{2,1,0:T(2,128)(2,1)} %reshape.170), calls=%async_computation.4 | async-start | bytes 720896 | tf_op jit(solution)/shard_map/all_to_all | solution.py:204
  263.1 13.7 %all-to-all-done.3 = bf16[64,2,1408]{2,1,0:T(2,128)(2,1)S(1)} async-done(((bf16[64,2,1408]{2,1,0:T(2,128)(2,1)}), bf16[64,2,1408]{2,1,0:T(2,128)(2,1)S(1)}, u32[]{:S(2)}, u32[]{:S(2)}) %all-to-all-start.3) | async-done | bytes 360480 | tf_op jit(solution)/shard_map/all_to_all | solution.py:204
  (108 shorter events, 39.4 us)
Async XLA Ops:
  8.8 32.4 %all-to-all-start = ((bf16[16,4,1920]{2,1,0:T(4,128)(2,1)}), bf16[16,4,1920]{2,1,0:T(4,128)(2,1)S(1)}, u32[]{:S(2)}, u32[]{:S(2)}) async-start(bf16[16,4,1920]{2,1,0:T(4,128)(2,1)} %broadcast_in_dim.8), calls=%async_computation | async-start | bytes 491520 | tf_op jit(solution)/shard_map/all_to_all | solution.py:102
  28.2 119.1 %all-gather.3.cloned.1.call-start = ((), (), s32[]{:S(2)}) async-start(), calls=%async_computation.8 | async-start | bytes 5292032 | tf_op jit(solution)/shard_map/all_gather | solution.py:111
  72.4 8.5 %copy-start.2 = (bf16[1,128,4096]{2,1,0:T(8,128)(2,1)S(1)}, bf16[1,128,4096]{2,1,0:T(8,128)(2,1)}, u32[]{:S(2)}) copy-start(bf16[1,128,4096]{2,1,0:T(8,128)(2,1)} %param.11) | copy-start | bytes 3145732
  73.3 8.5 %copy-start = (bf16[1,4096,128]{2,1,0:T(8,128)(2,1)S(1)}, bf16[1,4096,128]{2,1,0:T(8,128)(2,1)}, u32[]{:S(2)}) copy-start(bf16[1,4096,128]{2,1,0:T(8,128)(2,1)} %param.9) | copy-start | bytes 3145732
  73.4 8.5 %copy-start.1 = (bf16[1,4096,128]{2,1,0:T(8,128)(2,1)S(1)}, bf16[1,4096,128]{2,1,0:T(8,128)(2,1)}, u32[]{:S(2)}) copy-start(bf16[1,4096,128]{2,1,0:T(8,128)(2,1)} %param.10) | copy-start | bytes 3145732
  74.7 31.6 %all-to-all-start.2 = ((bf16[16,16,1792]{2,1,0:T(8,128)(2,1)}), bf16[16,16,1792]{2,1,0:T(8,128)(2,1)}, u32[]{:S(2)}, u32[]{:S(2)}) async-start(bf16[16,16,1792]{2,1,0:T(8,128)(2,1)} %bitcast.128), calls=%async_computation.2 | async-start | bytes 1835008 | tf_op jit(solution)/shard_map/all_to_all | solution.py:123
  80.8 160.1 %reduce-scatter.2.cloned.1.call-start = ((), (), s32[]{:S(2)}) async-start(), calls=%async_computation.7 | async-start | bytes 6127616 | tf_op jit(solution)/shard_map/reduce_scatter | solution.py:163
  107.5 14.5 %collective-permute-start.1 = (bf16[256,896]{1,0:T(8,128)(2,1)S(1)}, bf16[256,896]{1,0:T(8,128)(2,1)S(1)}, u32[]{:S(2)}, u32[]{:S(2)}) collective-permute-start(bf16[256,896]{1,0:T(8,128)(2,1)S(1)} %get-tuple-element.24), channel_id=1, source_target_pairs={{0,48},{16,0},{32,16},{48,32},{1,49},{17,1},{33,17},{49,33},{2,50}... | collective-permute-start | bytes 1376264 | tf_op jit(solution)/shard_map/ppermute | solution.py:126
  110.3 15.7 %collective-permute-start.2 = (bf16[256,896]{1,0:T(8,128)(2,1)S(1)}, bf16[256,896]{1,0:T(8,128)(2,1)S(1)}, u32[]{:S(2)}, u32[]{:S(2)}) collective-permute-start(bf16[256,896]{1,0:T(8,128)(2,1)S(1)} %get-tuple-element.23), channel_id=1, source_target_pairs={{0,16},{16,32},{32,48},{48,0},{1,17},{17,33},{33,49},{49,1},{2,18}... | collective-permute-start | bytes 1376264 | tf_op jit(solution)/shard_map/ppermute | solution.py:125
  113.5 23.0 %collective-permute-start = (bf16[256,896]{1,0:T(8,128)(2,1)S(1)}, bf16[256,896]{1,0:T(8,128)(2,1)S(1)}, u32[]{:S(2)}, u32[]{:S(2)}) collective-permute-start(bf16[256,896]{1,0:T(8,128)(2,1)S(1)} %get-tuple-element.23), channel_id=1, source_target_pairs={{0,48},{16,0},{32,16},{48,32},{1,49},{17,1},{33,17},{49,33},{2,50}... | collective-permute-start | bytes 1376264 | tf_op jit(solution)/shard_map/ppermute | solution.py:128
  117.4 18.4 %collective-permute-start.5 = (bf16[256,896]{1,0:T(8,128)(2,1)S(1)}, bf16[256,896]{1,0:T(8,128)(2,1)S(1)}, u32[]{:S(2)}, u32[]{:S(2)}) collective-permute-start(bf16[256,896]{1,0:T(8,128)(2,1)S(1)} %get-tuple-element.24), channel_id=1, source_target_pairs={{0,16},{16,32},{32,48},{48,0},{1,17},{17,33},{33,49},{49,1},{2,18}... | collective-permute-start | bytes 1376264 | tf_op jit(solution)/shard_map/ppermute | solution.py:127
  122.0 18.6 %collective-permute-start.4 = (bf16[256,896]{1,0:T(8,128)(2,1)S(1)}, bf16[256,896]{1,0:T(8,128)(2,1)S(1)}, u32[]{:S(2)}, u32[]{:S(2)}) collective-permute-start(bf16[256,896]{1,0:T(8,128)(2,1)S(1)} %collective-permute-done.1), channel_id=1, source_target_pairs={{0,48},{16,0},{32,16},{48,32},{1,49},{17,1},{33,17},{49,33},{2,50}... | collective-permute-start | bytes 1376264 | tf_op jit(solution)/shard_map/ppermute | solution.py:130
  126.0 18.7 %collective-permute-start.3 = (bf16[256,896]{1,0:T(8,128)(2,1)S(1)}, bf16[256,896]{1,0:T(8,128)(2,1)S(1)}, u32[]{:S(2)}, u32[]{:S(2)}) collective-permute-start(bf16[256,896]{1,0:T(8,128)(2,1)S(1)} %collective-permute-done.2), channel_id=1, source_target_pairs={{0,16},{16,32},{32,48},{48,0},{1,17},{17,33},{33,49},{49,1},{2,18}... | collective-permute-start | bytes 1376264 | tf_op jit(solution)/shard_map/ppermute | solution.py:129
  158.8 0.9 copy-start.3
  162.5 14.6 %collective-permute-start.6 = (bf16[256,640]{1,0:T(8,128)(2,1)S(1)}, bf16[256,640]{1,0:T(8,128)(2,1)S(1)}, u32[]{:S(2)}, u32[]{:S(2)}) collective-permute-start(bf16[256,640]{1,0:T(8,128)(2,1)S(1)} %fusion.1), channel_id=1, source_target_pairs={{0,16},{16,32},{32,48},{48,0},{1,17},{17,33},{33,49},{49,1},{2,18}... | collective-permute-start | bytes 983048 | tf_op jit(solution)/shard_map/ppermute | solution.py:185
  165.1 23.2 %collective-permute-start.8 = (bf16[256,640]{1,0:T(8,128)(2,1)S(1)}, bf16[256,640]{1,0:T(8,128)(2,1)}, u32[]{:S(2)}, u32[]{:S(2)}) collective-permute-start(bf16[256,640]{1,0:T(8,128)(2,1)S(1)} %fusion.2), channel_id=1, source_target_pairs={{0,48},{16,0},{32,16},{48,32},{1,49},{17,1},{33,17},{49,33},{2,50}... | collective-permute-start | bytes 983048 | tf_op jit(solution)/shard_map/ppermute | solution.py:188
  170.4 19.0 %collective-permute-start.9 = (bf16[256,640]{1,0:T(8,128)(2,1)S(1)}, bf16[256,640]{1,0:T(8,128)(2,1)S(1)}, u32[]{:S(2)}, u32[]{:S(2)}) collective-permute-start(bf16[256,640]{1,0:T(8,128)(2,1)S(1)} %fusion.3), channel_id=1, source_target_pairs={{0,16},{16,32},{32,48},{48,0},{1,17},{17,33},{33,49},{49,1},{2,18}... | collective-permute-start | bytes 983048 | tf_op jit(solution)/shard_map/ppermute | solution.py:187
  172.3 10.1 %collective-permute-start.10 = (bf16[256,640]{1,0:T(8,128)(2,1)S(1)}, bf16[256,640]{1,0:T(8,128)(2,1)S(1)}, u32[]{:S(2)}, u32[]{:S(2)}) collective-permute-start(bf16[256,640]{1,0:T(8,128)(2,1)S(1)} %fusion.4), channel_id=1, source_target_pairs={{0,48},{16,0},{32,16},{48,32},{1,49},{17,1},{33,17},{49,33},{2,50}... | collective-permute-start | bytes 983048 | tf_op jit(solution)/shard_map/ppermute | solution.py:186
  177.3 10.9 %collective-permute-start.7 = (bf16[256,640]{1,0:T(8,128)(2,1)S(1)}, bf16[256,640]{1,0:T(8,128)(2,1)S(1)}, u32[]{:S(2)}, u32[]{:S(2)}) collective-permute-start(bf16[256,640]{1,0:T(8,128)(2,1)S(1)} %add_convert_fusion.3), channel_id=1, source_target_pairs={{0,16},{16,32},{32,48},{48,0},{1,17},{17,33},{33,49},{49,1},{2,18}... | collective-permute-start | bytes 983048 | tf_op jit(solution)/shard_map/ppermute | solution.py:189
  182.6 10.1 %collective-permute-start.11 = (bf16[256,640]{1,0:T(8,128)(2,1)S(1)}, bf16[256,640]{1,0:T(8,128)(2,1)S(1)}, u32[]{:S(2)}, u32[]{:S(2)}) collective-permute-start(bf16[256,640]{1,0:T(8,128)(2,1)S(1)} %add_convert_fusion.1), channel_id=1, source_target_pairs={{0,48},{16,0},{32,16},{48,32},{1,49},{17,1},{33,17},{49,33},{2,50}... | collective-permute-start | bytes 983048 | tf_op jit(solution)/shard_map/ppermute | solution.py:190
  221.3 22.3 %all-to-all-start.5 = ((bf16[16,4,1280]{2,1,0:T(4,128)(2,1)}), bf16[16,4,1280]{2,1,0:T(4,128)(2,1)S(1)}, u32[]{:S(2)}, u32[]{:S(2)}) async-start(bf16[16,4,1280]{2,1,0:T(4,128)(2,1)} %all_to_all.55), calls=%async_computation.6 | async-start | bytes 327680 | tf_op jit(solution)/shard_map/all_to_all | solution.py:202
  243.6 33.2 %all-to-all-start.3 = ((bf16[64,2,1408]{2,1,0:T(2,128)(2,1)}), bf16[64,2,1408]{2,1,0:T(2,128)(2,1)S(1)}, u32[]{:S(2)}, u32[]{:S(2)}) async-start(bf16[64,2,1408]{2,1,0:T(2,128)(2,1)} %reshape.170), calls=%async_computation.4 | async-start | bytes 720896 | tf_op jit(solution)/shard_map/all_to_all | solution.py:204
Sparse Core Ops, SparseCore 0:
  73.3 66.8 all-gather.2
  159.0 81.9 reduce-scatter.1
